TPU v7x, 512 devices: a whole 4x4x16 slice. The times are simulated.
512 devices in a mesh: dp: 16 (over y_lo, x, core), code: 32 (over y_hi, z).
Axes of the slice: x: 4, y: 4 (y_hi: 2, y_lo: 2; y = y_hi * 2 + y_lo), z: 16, core: 2. Of those that a mesh axis runs over, the one named last changes fastest.
Arguments:
- features: bfloat16 [65536, 768], P('dp'), may hold values from -8 to 8
- centroids: bfloat16 [131072, 768], P(('code', 'dp')), may hold values from -4.7 to 4.7
- block_lists: int32 [128, 32], P('dp'), may hold values from 0 to 511, as said below
Outputs:
- new_centroids: bfloat16 [131072, 768], P(('code', 'dp'))
- column_mass: float32 [131072], P(('code', 'dp'))
Inputs may be any that keep to these rules, and one draw needn't show every extreme that they name: Let i = b // 8 for feature block b. Slot s of block_lists[b] names a block s * 16 + (i + e) mod 16 with e one of -1, 0, 1; in every slot, the 8 feature blocks with the same i together name all three such blocks.
All inputs are finite; a program needn't handle non-finite values.
Results may differ from a plain program's by a relative error of at most 0.0055.
The roundings to bfloat16 on the way count: a program that leaves them out, or rounds other values in their place, can miss the bound.
Values may be sent and summed in bfloat16 or wider, within the bound.
A program may use at most 64 MiB of HBM per device.

v0:
```python
import jax
import jax.numpy as jnp
from jax import lax
from jax.sharding import PartitionSpec as P

ROUNDS = 3


SOFTMAX_TEMP = 12.0
MASKED_LOGIT = -1e30


def with_halo(cells, sides, width):
    for axis, dim in sides:
        count = lax.axis_size(axis)
        head = lax.slice_in_dim(cells, 0, width, axis=dim)
        tail = lax.slice_in_dim(cells, cells.shape[dim] - width, cells.shape[dim], axis=dim)
        cells = jnp.concatenate(
            [
                lax.ppermute(tail, axis, [(i, (i + 1) % count) for i in range(count)]),
                cells,
                lax.ppermute(head, axis, [((i + 1) % count, i) for i in range(count)]),
            ],
            axis=dim,
        )
    return cells


def local(features, centroids, block_lists):
    dp_count = lax.axis_size("dp")
    code_count = lax.axis_size("code")
    row_count = features.shape[0]
    block_size = centroids.shape[0]
    width = centroids.shape[1]
    block_count = block_lists.shape[0]
    block_rows = row_count // block_count
    dp_index = lax.axis_index("dp")
    code_index = lax.axis_index("code")
    feat_blocks = features.reshape(block_count, block_rows, width)
    listed_ids = lax.dynamic_slice_in_dim(block_lists, code_index, 1, 1)[:, 0]
    owner_dp = listed_ids % dp_count
    window_pos = (owner_dp - dp_index + 1) % dp_count
    owner_match = owner_dp[:, None] == jnp.arange(dp_count, dtype=jnp.int32)[None, :]
    owner_hot = owner_match.astype(jnp.float32)
    window_hot = (window_pos[:, None] == jnp.arange(3, dtype=jnp.int32)[None, :]).astype(
        jnp.float32
    )
    window = with_halo(centroids, (("dp", 0),), block_size)
    picked = window.reshape(3, block_size, width)[window_pos]
    centroid_squared_norm = jnp.sum(jnp.square(picked.astype(jnp.float32)), axis=2)
    inner_product = jnp.einsum(
        "frd,fkd->frk", feat_blocks, picked, preferred_element_type=jnp.float32
    ).astype(jnp.bfloat16)
    assignment_logits = (
        2.0 * inner_product.astype(jnp.float32) - centroid_squared_norm[:, None, :]
    ) / SOFTMAX_TEMP
    log_target = jnp.log(jnp.float32(row_count) / jnp.float32(block_size * code_count))

    def row_potential(col_pick):
        shifted = assignment_logits + col_pick[:, None, :]
        local_peak = jnp.max(shifted, axis=2)
        row_peak = lax.pmax(local_peak, "code")
        local_total = jnp.sum(jnp.exp(shifted - row_peak[:, :, None]), axis=2)
        row_total = lax.psum(local_total, "code")
        return -(row_peak + jnp.log(row_total))

    col_pick = jnp.zeros((block_count, block_size), jnp.float32)
    for sweep_index in range(ROUNDS):
        row_pot = row_potential(col_pick)
        col_shifted = assignment_logits + row_pot[:, :, None]
        block_peak = jnp.max(col_shifted, axis=1)
        group_peak = jnp.max(
            jnp.where(owner_match[:, :, None], block_peak[:, None, :], MASKED_LOGIT), axis=0
        )
        col_peak = lax.pmax(group_peak, "dp")
        own_peak = col_peak[owner_dp]
        block_total = jnp.sum(jnp.exp(col_shifted - own_peak[:, None, :]), axis=1)
        col_total = lax.psum(
            jnp.sum(jnp.where(owner_match[:, :, None], block_total[:, None, :], 0.0), axis=0), "dp"
        )
        col_pick = (log_target - (col_peak + jnp.log(col_total)))[owner_dp]
    row_pot = row_potential(col_pick)
    weights = jnp.exp(assignment_logits + row_pot[:, :, None] + col_pick[:, None, :])
    weight_low = weights.astype(jnp.bfloat16)
    numer_block = jnp.einsum(
        "frk,frd->fkd", weight_low, feat_blocks, preferred_element_type=jnp.float32
    )
    numer_window = jnp.einsum(
        "fp,fkd->pkd", window_hot, numer_block, precision=lax.Precision.HIGHEST
    )
    numer_low = numer_window.reshape(3 * block_size, width).astype(jnp.bfloat16)
    rims = with_halo(numer_low, (("dp", 0),), block_size)
    numer_own = (
        rims[:block_size].astype(jnp.float32)
        + rims[2 * block_size : 3 * block_size].astype(jnp.float32)
        + rims[4 * block_size :].astype(jnp.float32)
    )
    mass_block = jnp.sum(weights, axis=1)
    mass_group = jnp.einsum("fo,fk->ok", owner_hot, mass_block, precision=lax.Precision.HIGHEST)
    mass_low = lax.optimization_barrier(mass_group.astype(jnp.bfloat16)).astype(jnp.float32)
    mass_all = lax.psum(mass_low, "dp")
    mass_own = lax.dynamic_slice_in_dim(mass_all, dp_index, 1, 0)[0]
    new_centroids = (numer_own / mass_own[:, None]).astype(jnp.bfloat16)
    return (new_centroids, mass_own)


def solution(mesh):
    in_specs = (P("dp", None), P(("code", "dp"), None), P("dp", None))
    out_specs = (P(("code", "dp"), None), P(("code", "dp")))
    return jax.shard_map(local, mesh=mesh, in_specs=in_specs, out_specs=out_specs, check_vma=False)
```

profile of v0, /device:TPU:1, one launch (start us, length us, event | category | flops | bytes accessed | tf_op | source)
XLA Modules:
  0.0 1590.0 jit_solution(14726941143153623671)
XLA Ops:
  0.6 4.5 collective-permute-start
  5.1 6.2 collective-permute-start.1
  12.4 2.4 collective-permute-done.1
  15.8 2.4 gather_fusion
  18.2 2.6 multiply_reduce_fusion
  20.8 5.6 bitcast_reduce_fusion
  26.4 126.2 %pmax.49 = f32[8,512]{1,0:T(8,128)S(1)} all-reduce(f32[8,512]{1,0:T(8,128)S(1)} %get-tuple-element.9), channel_id=1, replica_groups=mesh['dp'=16,'code'=32] {'code'}, use_global_device_ids=true, to_apply=%region_2.3 | all-reduce | flops 4096 | bytes 32768 | tf_op jit(solution)/shard_map/pmax | solution.py:62
  153.9 114.8 %psum.56 = f32[8,512]{1,0:T(8,128)S(1)} all-reduce(f32[8,512]{1,0:T(8,128)S(1)} %fusion.3), channel_id=1, replica_groups=mesh['dp'=16,'code'=32] {'code'}, use_global_device_ids=true, to_apply=%region_4.5 | all-reduce | flops 4096 | bytes 32768 | tf_op jit(solution)/shard_map/psum | solution.py:64
  270.0 104.9 %pmax.50 = f32[16,256]{1,0:T(8,128)S(1)} all-reduce(f32[16,256]{1,0:T(8,128)S(1)} %select_reduce_fusion.5), channel_id=1, replica_groups=mesh['dp'=16,'code'=32] {'dp'}, use_global_device_ids=true, to_apply=%region_7.8 | all-reduce | flops 4096 | bytes 32768 | tf_op jit(solution)/shard_map/pmax | solution.py:75
  377.3 52.9 %psum.57 = f32[16,256]{1,0:T(8,128)S(1)} all-reduce(f32[16,256]{1,0:T(8,128)S(1)} %select_reduce_fusion.4), channel_id=1, replica_groups=mesh['dp'=16,'code'=32] {'dp'}, use_global_device_ids=true, to_apply=%region_10.11 | all-reduce | flops 4096 | bytes 32768 | tf_op jit(solution)/shard_map/psum | solution.py:78
  431.8 115.0 %pmax.51 = f32[8,512]{1,0:T(8,128)S(1)} all-reduce(f32[8,512]{1,0:T(8,128)S(1)} %fusion.7), channel_id=1, replica_groups=mesh['dp'=16,'code'=32] {'code'}, use_global_device_ids=true, to_apply=%region_12.13 | all-reduce | flops 4096 | bytes 32768 | tf_op jit(solution)/shard_map/pmax | solution.py:62
  548.2 115.1 %psum.58 = f32[8,512]{1,0:T(8,128)S(1)} all-reduce(f32[8,512]{1,0:T(8,128)S(1)} %exponential_reduce_fusion.4), channel_id=1, replica_groups=mesh['dp'=16,'code'=32] {'code'}, use_global_device_ids=true, to_apply=%region_14.15 | all-reduce | flops 4096 | bytes 32768 | tf_op jit(solution)/shard_map/psum | solution.py:64
  664.6 107.6 %pmax.52 = f32[16,256]{1,0:T(8,128)S(1)} all-reduce(f32[16,256]{1,0:T(8,128)S(1)} %select_reduce_fusion.3), channel_id=1, replica_groups=mesh['dp'=16,'code'=32] {'dp'}, use_global_device_ids=true, to_apply=%region_17.18 | all-reduce | flops 4096 | bytes 32768 | tf_op jit(solution)/shard_map/pmax | solution.py:75
  774.5 53.1 %psum.59 = f32[16,256]{1,0:T(8,128)S(1)} all-reduce(f32[16,256]{1,0:T(8,128)S(1)} %select_reduce_fusion.2), channel_id=1, replica_groups=mesh['dp'=16,'code'=32] {'dp'}, use_global_device_ids=true, to_apply=%region_20.21 | all-reduce | flops 4096 | bytes 32768 | tf_op jit(solution)/shard_map/psum | solution.py:78
  829.1 115.0 %pmax.53 = f32[8,512]{1,0:T(8,128)S(1)} all-reduce(f32[8,512]{1,0:T(8,128)S(1)} %fusion.9), channel_id=1, replica_groups=mesh['dp'=16,'code'=32] {'code'}, use_global_device_ids=true, to_apply=%region_22.23 | all-reduce | flops 4096 | bytes 32768 | tf_op jit(solution)/shard_map/pmax | solution.py:62
  945.6 115.1 %psum.60 = f32[8,512]{1,0:T(8,128)S(1)} all-reduce(f32[8,512]{1,0:T(8,128)S(1)} %exponential_reduce_fusion.2), channel_id=1, replica_groups=mesh['dp'=16,'code'=32] {'code'}, use_global_device_ids=true, to_apply=%region_24.25 | all-reduce | flops 4096 | bytes 32768 | tf_op jit(solution)/shard_map/psum | solution.py:64
  1062.0 107.6 %pmax.54 = f32[16,256]{1,0:T(8,128)S(1)} all-reduce(f32[16,256]{1,0:T(8,128)S(1)} %select_reduce_fusion.1), channel_id=1, replica_groups=mesh['dp'=16,'code'=32] {'dp'}, use_global_device_ids=true, to_apply=%region_27.28 | all-reduce | flops 4096 | bytes 32768 | tf_op jit(solution)/shard_map/pmax | solution.py:75
  1171.9 52.9 %psum.61 = f32[16,256]{1,0:T(8,128)S(1)} all-reduce(f32[16,256]{1,0:T(8,128)S(1)} %select_reduce_fusion), channel_id=1, replica_groups=mesh['dp'=16,'code'=32] {'dp'}, use_global_device_ids=true, to_apply=%region_30.31 | all-reduce | flops 4096 | bytes 32768 | tf_op jit(solution)/shard_map/psum | solution.py:78
  1226.3 115.0 %pmax.55 = f32[8,512]{1,0:T(8,128)S(1)} all-reduce(f32[8,512]{1,0:T(8,128)S(1)} %fusion.11), channel_id=1, replica_groups=mesh['dp'=16,'code'=32] {'code'}, use_global_device_ids=true, to_apply=%region_32.33 | all-reduce | flops 4096 | bytes 32768 | tf_op jit(solution)/shard_map/pmax | solution.py:62
  1342.8 115.1 %psum.62 = f32[8,512]{1,0:T(8,128)S(1)} all-reduce(f32[8,512]{1,0:T(8,128)S(1)} %exponential_reduce_fusion), channel_id=1, replica_groups=mesh['dp'=16,'code'=32] {'code'}, use_global_device_ids=true, to_apply=%region_34.35 | all-reduce | flops 4096 | bytes 32768 | tf_op jit(solution)/shard_map/psum | solution.py:64
  1457.9 4.2 fusion.14
  1462.0 5.7 fusion.21
  1471.0 61.0 %collective-permute-start.3 = (bf16[256,768]{1,0:T(8,128)(2,1)}, bf16[256,768]{1,0:T(8,128)(2,1)S(1)}, u32[]{:S(2)}, u32[]{:S(2)}) collective-permute-start(bf16[256,768]{1,0:T(8,128)(2,1)} %bitcast.70), channel_id=1, source_target_pairs={{32,0},{64,32},{96,64},{128,96},{160,128},{192,160},{224,192},{256... | collective-permute-start | bytes 1179656 | tf_op jit(solution)/shard_map/ppermute | solution.py:22
  1535.9 52.2 %psum.63 = f32[16,256]{1,0:T(8,128)S(1)} all-reduce(bf16[16,256]{1,0:T(8,128)(2,1)S(1)} %convolution_convert_fusion.1), channel_id=1, replica_groups=mesh['dp'=16,'code'=32] {'dp'}, use_global_device_ids=true, to_apply=%region_36.37 | all-reduce | flops 4096 | bytes 24576 | tf_op jit(solution)/shard_map/psum | solution.py:101
  (50 shorter events, 32.1 us)
Async XLA Ops:
  0.6 11.8 collective-permute-start
  5.1 9.6 collective-permute-start.1
  1471.0 117.0 %collective-permute-start.3 = (bf16[256,768]{1,0:T(8,128)(2,1)}, bf16[256,768]{1,0:T(8,128)(2,1)S(1)}, u32[]{:S(2)}, u32[]{:S(2)}) collective-permute-start(bf16[256,768]{1,0:T(8,128)(2,1)} %bitcast.70), channel_id=1, source_target_pairs={{32,0},{64,32},{96,64},{128,96},{160,128},{192,160},{224,192},{256... | collective-permute-start | bytes 1179656 | tf_op jit(solution)/shard_map/ppermute | solution.py:22
  1532.0 56.0 %collective-permute-start.2 = (bf16[256,768]{1,0:T(8,128)(2,1)}, bf16[256,768]{1,0:T(8,128)(2,1)}, u32[]{:S(2)}, u32[]{:S(2)}) collective-permute-start(bf16[256,768]{1,0:T(8,128)(2,1)} %bitcast.69), channel_id=1, source_target_pairs={{0,32},{32,64},{64,96},{96,128},{128,160},{160,192},{192,224},{224... | collective-permute-start | bytes 1179656 | tf_op jit(solution)/shard_map/ppermute | solution.py:20
  1588.1 1.9 copy-start
where the time goes:
time: 1590 us
  blocking collectives  1460 us (92%)
  starting transfers between devices  73.6 us (5%)
  other arithmetic  27.6 us (2%)
    pmax x4, blocking collectives, row_potential(): row_peak = lax.pmax(local_peak, 'code')  471 us
    psum x4, blocking collectives, row_potential(): row_total = lax.psum(local_total, 'code')  460 us
    pmax x3, blocking collectives, local(): col_peak = lax.pmax(group_peak, 'dp')  320 us
    psum x3, blocking collectives, local(): lax.psum(jnp.sum(jnp.where(owner_match[:, :, None], block_total[:, None,...  159 us
    ppermute x2, starting transfers between devices, with_halo(): lax.ppermute(head, axis, [((i + 1) % count, i) for i in range(count)])  67.2 us
    psum x1, blocking collectives, local(): mass_all = lax.psum(mass_low, 'dp')  52.2 us
  transfers between devices with their start and end apart: 4, of which 1 were waited for; matrix products, arithmetic and copies ran while one was open for 0% of the time, Pallas kernels for 0%

commit v1 on v0

v1 whole, which is shorter than its diff:
```python
import functools
import math

import jax
import jax.numpy as jnp
from jax import lax
from jax.experimental import pallas as pl
from jax.experimental.pallas import tpu as pltpu
from jax.sharding import PartitionSpec as P

ROUNDS = 3
SOFTMAX_TEMP = 12.0
LOG2E = math.log2(math.e)
LOWEST = -3.0e38
LANES = 128
SUB = 8
PIECES = 3
MESH = pl.DeviceIdType.MESH


def kernel(
    n_dp,
    n_code,
    lists_ref,
    feat_hbm,
    cent_hbm,
    out_ref,
    mass_ref,
    feat,
    win,
    cells,
    row_b,
    col_b,
    peak,
    total,
    weight,
    lse_src,
    lse_in,
    row_src,
    row_in,
    col_src,
    col_l2,
    col_l1,
    col_r1,
    col_r2,
    mass_src,
    mass_in,
    num_src,
    num_in,
    num_own,
    feat_sem,
    own_sem,
    halo_send,
    halo_recv,
    lse_send,
    lse_recv,
    row_send,
    row_recv,
    col_send,
    col_recv,
    mass_send,
    mass_recv,
    num_send,
    num_recv,
):
    dp = lax.axis_index("dp")
    code = lax.axis_index("code")
    blocks = lists_ref.shape[0]
    rows = feat.shape[0]
    block_rows = rows // blocks
    block_tiles = block_rows // LANES
    tiles = rows // LANES
    size, width = win.shape[1], win.shape[2]
    halves = size // LANES
    piece = width // PIECES
    odd = lax.rem(dp, 2)

    def dp_at(step):
        return lax.rem(dp + (n_dp + step), n_dp)

    def place(b):
        return jnp.minimum(lax.rem(lists_ref[b, code] + (n_dp + 1) - dp, n_dp), 2)

    def feat_copy(b):
        span = pl.ds(b * block_rows, block_rows)
        return pltpu.make_async_copy(feat_hbm.at[span], feat.at[span], feat_sem.at[b])

    def remote(src, dst, send, recv, to_dp, to_code):
        return pltpu.make_async_remote_copy(
            src_ref=src,
            dst_ref=dst,
            send_sem=send,
            recv_sem=recv,
            device_id=(to_dp, to_code),
            device_id_type=MESH,
        )

    own_copy = pltpu.make_async_copy(cent_hbm, win.at[1], own_sem)
    own_copy.start()
    for b in range(blocks):
        feat_copy(b).start()

    barrier = pltpu.get_barrier_semaphore()
    for step in (-2, -1, 1, 2):
        pl.semaphore_signal(
            barrier, inc=1, device_id=(dp_at(step), code), device_id_type=MESH
        )

    def greet(j, carry):
        to = lax.rem(code + 1 + j, n_code)
        pl.semaphore_signal(barrier, inc=1, device_id=(dp, to), device_id_type=MESH)
        return carry

    lax.fori_loop(0, n_code - 1, greet, 0)
    pl.semaphore_wait(barrier, n_code - 1 + 4)

    def side(s):
        return 2 * lax.rem(odd + s, 2)

    def halo(s):
        w = side(s)
        return remote(
            cent_hbm,
            win.at[2 - w],
            halo_send.at[s],
            halo_recv.at[1 - w // 2],
            dp_at(w - 1),
            code,
        )

    halo(0).start()
    halo(1).start()
    own_copy.wait()
    for s in range(2):
        halo(s).wait_send()
    for s in range(2):
        remote(cent_hbm, win.at[2 * s], halo_send.at[s], halo_recv.at[s], dp, code).wait_recv()

    eye = lax.broadcasted_iota(jnp.int32, (LANES, LANES), 0) == lax.broadcasted_iota(
        jnp.int32, (LANES, LANES), 1
    )

    def to_lanes(column):
        square = column.reshape(3 * halves, LANES, LANES)
        flat = jnp.sum(jnp.where(eye[None], square, 0.0), axis=1)
        return flat.reshape(3, halves, LANES)

    def to_column(row):
        square = jnp.where(eye, jnp.broadcast_to(row, (LANES, LANES)), 0.0)
        return jnp.broadcast_to(jnp.sum(square, axis=1, keepdims=True), (LANES, LANES))

    def norms(w, carry):
        wide = win[w].astype(jnp.float32)
        norm = jnp.sum(wide * wide, axis=1, keepdims=True)
        col_b[w] = jnp.broadcast_to(norm * (-LOG2E / SOFTMAX_TEMP), (size, LANES))
        return carry

    lax.fori_loop(0, 3, norms, 0)

    def score(b, carry):
        feat_copy(b).wait()
        inner = lax.dot_general(
            win[place(b)],
            feat[pl.ds(pl.multiple_of(b * block_rows, block_rows), block_rows), :],
            (((1,), (1,)), ((), ())),
            preferred_element_type=jnp.float32,
        )
        scaled = inner.astype(jnp.bfloat16).astype(jnp.float32) * (2.0 * LOG2E / SOFTMAX_TEMP)
        for t in range(block_tiles):
            cells[b * block_tiles + t] = scaled[:, t * LANES : (t + 1) * LANES]
        return carry

    lax.fori_loop(0, blocks, score, 0)

    group = 4

    def row_update(r):
        def some_tiles(step, carry):
            ids = [lax.rem(code + 1 + step * group + u, n_code) for u in range(group)]
            for d in ids:
                x = cells[d] + col_b[place(d // block_tiles)]
                x = x.reshape(size // SUB, SUB, LANES)
                m8 = jnp.max(x, axis=0)
                s8 = jnp.sum(jnp.exp2(x - m8[None]), axis=0)
                m = jnp.max(m8, axis=0, keepdims=True)
                s = jnp.sum(s8 * jnp.exp2(m8 - m), axis=0, keepdims=True)
                lse_src[r, d] = m + jnp.log2(s)
            for u, d in enumerate(ids):

                @pl.when(step * group + u < n_code - 1)
                def _():
                    remote(
                        lse_src.at[r, d], lse_in.at[r, code], lse_send.at[r], lse_recv.at[r], dp, d
                    ).start()

            return carry

        lax.fori_loop(0, tiles // group, some_tiles, 0)
        lse_in[r, code] = lse_src[r, code]
        some = pl.ds(0, n_code - 1)
        all_in = remote(
            lse_src.at[r, some], lse_in.at[r, some], lse_send.at[r], lse_recv.at[r], dp, code
        )
        all_in.wait_recv()
        parts = lse_in[r]
        m = jnp.max(parts, axis=0)
        s = jnp.sum(jnp.exp2(parts - m[None]), axis=0)
        value = -(m + jnp.log2(s))
        row_src[r] = value
        row_in[r, code] = value

        def tell(j, carry):
            to = lax.rem(code + 1 + j, n_code)
            remote(
                row_src.at[r], row_in.at[r, code], row_send.at[r], row_recv.at[r], dp, to
            ).start()
            return carry

        lax.fori_loop(0, n_code - 1, tell, 0)
        all_in.wait_send()
        all_rows = remote(
            lse_src.at[r, some], row_in.at[r, some], row_send.at[r], row_recv.at[r], dp, code
        )
        all_rows.wait_recv()
        row_b[...] = jnp.broadcast_to(row_in[r], row_b.shape)
        all_rows.wait_send()

    def col_update(r, target):
        def some_cols(j, carry):
            span = pl.ds(pl.multiple_of(j * SUB, SUB), SUB)
            x = cells[:, span, :] + row_b[...]
            x = x.reshape(blocks, block_tiles, SUB, LANES)
            places = [jnp.full((SUB, LANES), place(b), jnp.int32) for b in range(blocks)]
            tops = [jnp.max(x[b], axis=0) for b in range(blocks)]
            peaks = []
            for w in range(3):
                held = [jnp.where(places[b] == w, tops[b], LOWEST) for b in range(blocks)]
                peaks.append(functools.reduce(jnp.maximum, held))
            sums = []
            for b in range(blocks):
                top = jnp.where(
                    places[b] == 0, peaks[0], jnp.where(places[b] == 1, peaks[1], peaks[2])
                )
                sums.append(jnp.sum(jnp.exp2(x[b] - top[None]), axis=0))
            for w in range(3):
                held = [jnp.where(places[b] == w, sums[b], 0.0) for b in range(blocks)]
                peak[w, span, :] = peaks[w]
                total[w, span, :] = functools.reduce(jnp.add, held)
            return carry

        lax.fori_loop(0, size // SUB, some_cols, 0)
        m = jnp.max(peak[...], axis=2, keepdims=True)
        s = jnp.sum(total[...] * jnp.exp2(peak[...] - m), axis=2, keepdims=True)
        mine = to_lanes(jnp.broadcast_to(m, peak.shape)) + jnp.log2(
            to_lanes(jnp.broadcast_to(s, total.shape))
        )
        col_src[r] = mine
        copies = [
            remote(
                col_src.at[r, pl.ds(start, count)],
                there.at[r],
                col_send.at[r, slot],
                col_recv.at[r, slot],
                dp_at(step),
                code,
            )
            for slot, (step, start, count, there) in enumerate(
                ((-2, 0, 1, col_r2), (2, 2, 1, col_l2), (-1, 0, 2, col_r1), (1, 1, 2, col_l1))
            )
        ]
        for copy in copies:
            copy.start()
        for copy in copies:
            copy.wait_recv()
        l1, r1 = col_l1[r], col_r1[r]
        sets = (
            (col_l2[r, 0], l1[0], mine[0]),
            (l1[1], mine[1], r1[0]),
            (mine[2], r1[1], col_r2[r, 0]),
        )
        for w, terms in enumerate(sets):
            m = functools.reduce(jnp.maximum, terms)
            s = functools.reduce(jnp.add, [jnp.exp2(term - m) for term in terms])
            value = target - (m + jnp.log2(s))
            for h in range(halves):
                col_b[w, h * LANES : (h + 1) * LANES, :] = to_column(value[h : h + 1])
        for copy in copies:
            copy.wait_send()

    target = math.log2((rows * n_dp) / (size * n_dp * n_code))

    def sweep(r, carry):
        row_update(r)
        col_update(r, target)
        return carry

    lax.fori_loop(0, ROUNDS, sweep, 0)
    row_update(ROUNDS)

    pack = 2 * SUB

    def weigh(j, carry):
        span = pl.ds(pl.multiple_of(j * pack, pack), pack)
        sums = [jnp.zeros((2, SUB, LANES), jnp.float32) for w in range(3)]
        for b in range(blocks):
            at = place(b)
            at_b = jnp.full((2, SUB, LANES), at, jnp.int32)
            g = col_b[at, span, :].reshape(2, SUB, LANES)
            here = jnp.zeros((2, SUB, LANES), jnp.float32)
            for t in range(block_tiles):
                d = b * block_tiles + t
                x = cells[d, span, :].reshape(2, SUB, LANES) + row_b[d][None] + g
                value = jnp.exp2(x)
                here = here + value
                for w in range(3):
                    kept = jnp.where(at_b == w, value, 0.0).reshape(pack, LANES)
                    weight[w, span, d * LANES : (d + 1) * LANES] = kept.astype(jnp.bfloat16)
            for w in range(3):
                sums[w] = sums[w] + jnp.where(at_b == w, here, 0.0)
        for w in range(3):
            total[w, span, :] = sums[w].reshape(pack, LANES)
        return carry

    lax.fori_loop(0, size // pack, weigh, 0)

    mass = jnp.sum(total[...], axis=2, keepdims=True)
    mass = to_lanes(jnp.broadcast_to(mass, total.shape))
    mass_src[...] = mass.astype(jnp.bfloat16).astype(jnp.float32)
    mass_copies = [
        remote(
            mass_src.at[pl.ds(2 * s, 1)],
            mass_in.at[1 - s],
            mass_send.at[s],
            mass_recv.at[1 - s],
            dp_at(2 * s - 1),
            code,
        )
        for s in range(2)
    ]
    for copy in mass_copies:
        copy.start()

    def columns(n):
        return pl.ds(pl.multiple_of(n * piece, piece), piece)

    def numerator(w, n):
        return jnp.dot(weight[w], feat[:, columns(n)], preferred_element_type=jnp.float32)

    def num_copy(s, n):
        w = side(s)
        return remote(
            num_src.at[s, n],
            num_in.at[1 - w // 2, n],
            num_send.at[s, n],
            num_recv.at[1 - w // 2, n],
            dp_at(w - 1),
            code,
        )

    def give(q, carry):
        s, n = q // PIECES, lax.rem(q, PIECES)
        num_src[s, n] = numerator(side(s), n).astype(jnp.bfloat16)
        num_copy(s, n).start()
        return carry

    lax.fori_loop(0, 2 * PIECES, give, 0)

    def keep(n, carry):
        num_own[n] = numerator(1, n).astype(jnp.bfloat16).astype(jnp.float32)
        return carry

    lax.fori_loop(0, PIECES, keep, 0)

    for s in range(2):
        remote(
            mass_src.at[pl.ds(0, 1)], mass_in.at[s], mass_send.at[s], mass_recv.at[s], dp, code
        ).wait_recv()
    for copy in mass_copies:
        copy.wait_send()
    mass_all = mass_in[0, 0] + mass_src[1] + mass_in[1, 0]
    mass_ref[...] = mass_all
    for h in range(halves):
        peak[0, h * LANES : (h + 1) * LANES, :] = to_column(mass_all[h : h + 1])

    def finish(n, carry):
        for s in range(2):
            remote(
                num_src.at[s, n], num_in.at[s, n], num_send.at[s, n], num_recv.at[s, n], dp, code
            ).wait()
        whole = (
            num_in[0, n].astype(jnp.float32) + num_own[n] + num_in[1, n].astype(jnp.float32)
        )
        divisor = jnp.concatenate([peak[0]] * (piece // LANES), axis=1)
        out_ref[:, columns(n)] = (whole / divisor).astype(jnp.bfloat16)
        return carry

    lax.fori_loop(0, PIECES, finish, 0)


def solution(mesh):
    n_dp, n_code = mesh.shape["dp"], mesh.shape["code"]

    def local(features, centroids, block_lists):
        rows, width = features.shape
        size = centroids.shape[0]
        tiles = rows // LANES
        halves = size // LANES
        piece = width // PIECES
        updates = ROUNDS + 1
        f32, bf16 = jnp.float32, jnp.bfloat16
        dma = pltpu.SemaphoreType.DMA
        new_centroids, mass = pl.pallas_call(
            functools.partial(kernel, n_dp, n_code),
            out_shape=(
                jax.ShapeDtypeStruct((size, width), bf16),
                jax.ShapeDtypeStruct((halves, LANES), f32),
            ),
            in_specs=[
                pl.BlockSpec(memory_space=pltpu.SMEM),
                pl.BlockSpec(memory_space=pl.ANY),
                pl.BlockSpec(memory_space=pl.ANY),
            ],
            out_specs=(
                pl.BlockSpec(memory_space=pltpu.VMEM),
                pl.BlockSpec(memory_space=pltpu.VMEM),
            ),
            scratch_shapes=[
                pltpu.VMEM((rows, width), bf16),
                pltpu.VMEM((3, size, width), bf16),
                pltpu.VMEM((tiles, size, LANES), f32),
                pltpu.VMEM((tiles, SUB, LANES), f32),
                pltpu.VMEM((3, size, LANES), f32),
                pltpu.VMEM((3, size, LANES), f32),
                pltpu.VMEM((3, size, LANES), f32),
                pltpu.VMEM((3, size, rows), bf16),
                pltpu.VMEM((updates, tiles, 1, LANES), f32),
                pltpu.VMEM((updates, tiles, 1, LANES), f32),
                pltpu.VMEM((updates, 1, LANES), f32),
                pltpu.VMEM((updates, tiles, 1, LANES), f32),
                pltpu.VMEM((ROUNDS, 3, halves, LANES), f32),
                pltpu.VMEM((ROUNDS, 1, halves, LANES), f32),
                pltpu.VMEM((ROUNDS, 2, halves, LANES), f32),
                pltpu.VMEM((ROUNDS, 2, halves, LANES), f32),
                pltpu.VMEM((ROUNDS, 1, halves, LANES), f32),
                pltpu.VMEM((3, halves, LANES), f32),
                pltpu.VMEM((2, 1, halves, LANES), f32),
                pltpu.VMEM((2, PIECES, size, piece), bf16),
                pltpu.VMEM((2, PIECES, size, piece), bf16),
                pltpu.VMEM((PIECES, size, piece), f32),
                dma((block_lists.shape[0],)),
                dma,
                dma((2,)),
                dma((2,)),
                dma((updates,)),
                dma((updates,)),
                dma((updates,)),
                dma((updates,)),
                dma((ROUNDS, 4)),
                dma((ROUNDS, 4)),
                dma((2,)),
                dma((2,)),
                dma((2, PIECES)),
                dma((2, PIECES)),
            ],
            compiler_params=pltpu.CompilerParams(
                collective_id=0, has_side_effects=True, vmem_limit_bytes=56 * 1024 * 1024
            ),
            cost_estimate=pl.CostEstimate(
                flops=8 * rows * size * width,
                bytes_accessed=2 * (rows + 2 * size) * width,
                transcendentals=8 * rows * size,
            ),
            name="balanced_kmeans",
        )(block_lists, features, centroids)
        return new_centroids, mass.reshape(size)

    return jax.shard_map(
        local,
        mesh=mesh,
        in_specs=(P("dp", None), P(("code", "dp"), None), P("dp", None)),
        out_specs=(P(("code", "dp"), None), P(("code", "dp"))),
        check_vma=False,
    )
```

time: 1590 us -> 133 us (0.08)
  blocking collectives: 1460 us -> 0 us
  Pallas kernels: 0 us -> 129 us
  starting transfers between devices: 73.6 us -> 0 us
  other arithmetic: 27.6 us -> 0 us
    pmax x7 -> x0, blocking collectives: 791 us -> none  [the longest x4 471 us: row_potential(): row_peak = lax.pmax(local_peak, 'code')]
    psum x8 -> x0, blocking collectives: 671 us -> none  [the longest x4 460 us: row_potential(): row_total = lax.psum(local_total, 'code')]
    pallas_call x0 -> x1, Pallas kernels: none -> 129 us  [local(): pl.pallas_call(functools.partial(kernel, n_dp, n_code), out_shape=(jax.Sh...]
    ppermute x4 -> x0, starting transfers between devices: 73.6 us -> none  [the longest x2 67.2 us: with_halo(): lax.ppermute(head, axis, [((i + 1) % count, i) for i in range(count)])]
  transfers between devices with their start and end apart: 4 -> 0, of which waited for: 1 -> 0; matrix products, arithmetic and copies ran while one was open for 0% -> 0% of each run, Pallas kernels for 0% -> 0%
where the time goes in v1:
time: 133 us; the launch traced here: 132 us
  Pallas kernels  129 us (97%)
  local copies, waits for them, and re-layouts  2.96 us (2%)
    pallas_call x1, Pallas kernels, local(): pl.pallas_call(functools.partial(kernel, n_dp, n_code), out_shape=(jax.Sh...  129 us
    unnamed x2, local copies, waits for them, and re-layouts  2.96 us

profile of v1, /device:TPU:1, one launch (start us, length us, event | category | flops | bytes accessed | tf_op | source)
XLA Modules:
  0.0 132.4 jit_solution(3264897042983782940)
XLA Ops:
  0.6 128.8 %balanced_kmeans.1 = (bf16[256,768]{1,0:T(8,128)(2,1)}, f32[2,128]{1,0:T(2,128)}) custom-call(s32[8,32]{1,0:T(8,128)} %lists_ref.1, bf16[4096,768]{1,0:T(8,128)(2,1)} %feat_hbm.1, bf16[256,768]{1,0:T(8,128)(2,1)} %cent_hbm.1), custom_call_target="tpu_custom_call" | custom-call | flops 6442450944 | bytes 7077888 | tf_op jit(solution)/shard_map/balanced_kmeans/pallas_call | solution.py:412
  129.4 1.8 %copy.7 = bf16[256,768]{1,0:T(8,128)(2,1)} copy(bf16[256,768]{1,0:T(8,128)(2,1)} %get-tuple-element.8) | data formatting | bytes 786432
  131.2 1.2 copy.8

commit v2 on v1

--- a/solution.py
+++ b/solution.py
@@ -15,6 +15,8 @@
 LANES = 128
 SUB = 8
 PIECES = 3
+Z = 16
+NEAR = 4
 MESH = pl.DeviceIdType.MESH
 
 
@@ -24,7 +26,7 @@
     lists_ref,
     feat_hbm,
     cent_hbm,
-    out_ref,
+    whole_ref,
     mass_ref,
     feat,
     win,
@@ -36,6 +38,8 @@
     weight,
     lse_src,
     lse_in,
+    mid_src,
+    mid_in,
     row_src,
     row_in,
     col_src,
@@ -54,6 +58,8 @@
     halo_recv,
     lse_send,
     lse_recv,
+    mid_send,
+    mid_recv,
     row_send,
     row_recv,
     col_send,
@@ -75,6 +81,17 @@
     piece = width // PIECES
     odd = lax.rem(dp, 2)
 
+    y_hi, z = code // Z, lax.rem(code, Z)
+    quarter, near = z // NEAR, lax.rem(z, NEAR)
+    quarters, shares = Z // NEAR, NEAR * (n_code // Z)
+    share = y_hi * NEAR + near
+
+    def mate(other):
+        return (other // NEAR) * Z + quarter * NEAR + lax.rem(other, NEAR)
+
+    def far_mate(other):
+        return y_hi * Z + other * NEAR + near
+
     def dp_at(step):
         return lax.rem(dp + (n_dp + step), n_dp)
 
@@ -101,18 +118,18 @@
         feat_copy(b).start()
 
     barrier = pltpu.get_barrier_semaphore()
-    for step in (-2, -1, 1, 2):
+    for step in (-1, 1, -2, 2):
         pl.semaphore_signal(
             barrier, inc=1, device_id=(dp_at(step), code), device_id_type=MESH
         )
-
-    def greet(j, carry):
-        to = lax.rem(code + 1 + j, n_code)
+    for step in range(1, shares):
+        pl.semaphore_signal(
+            barrier, inc=1, device_id=(dp, mate((share + step) % shares)), device_id_type=MESH
+        )
+    for step in range(1, quarters):
+        to = far_mate((quarter + step) % quarters)
         pl.semaphore_signal(barrier, inc=1, device_id=(dp, to), device_id_type=MESH)
-        return carry
-
-    lax.fori_loop(0, n_code - 1, greet, 0)
-    pl.semaphore_wait(barrier, n_code - 1 + 4)
+    pl.semaphore_wait(barrier, 4 + shares - 1 + quarters - 1)
 
     def side(s):
         return 2 * lax.rem(odd + s, 2)
@@ -130,7 +147,14 @@
 
     halo(0).start()
     halo(1).start()
+
+    def norms(w):
+        wide = win[w].astype(jnp.float32)
+        norm = jnp.sum(wide * wide, axis=1, keepdims=True)
+        col_b[w] = jnp.broadcast_to(norm * (-LOG2E / SOFTMAX_TEMP), (size, LANES))
+
     own_copy.wait()
+    norms(1)
     for s in range(2):
         halo(s).wait_send()
     for s in range(2):
@@ -148,14 +172,6 @@
     def to_column(row):
         square = jnp.where(eye, jnp.broadcast_to(row, (LANES, LANES)), 0.0)
         return jnp.broadcast_to(jnp.sum(square, axis=1, keepdims=True), (LANES, LANES))
-
-    def norms(w, carry):
-        wide = win[w].astype(jnp.float32)
-        norm = jnp.sum(wide * wide, axis=1, keepdims=True)
-        col_b[w] = jnp.broadcast_to(norm * (-LOG2E / SOFTMAX_TEMP), (size, LANES))
-        return carry
-
-    lax.fori_loop(0, 3, norms, 0)
 
     def score(b, carry):
         feat_copy(b).wait()
@@ -171,59 +187,86 @@
         return carry
 
     lax.fori_loop(0, blocks, score, 0)
-
-    group = 4
+    norms(0)
+    norms(2)
+
+    def row_block(r, b):
+        bias = col_b[place(b)]
+        for t in range(block_tiles):
+            x = (cells[b * block_tiles + t] + bias).reshape(size // SUB, SUB, LANES)
+            m8 = jnp.max(x, axis=0)
+            s8 = jnp.sum(jnp.exp2(x - m8[None]), axis=0)
+            m = jnp.max(m8, axis=0, keepdims=True)
+            s = jnp.sum(s8 * jnp.exp2(m8 - m), axis=0, keepdims=True)
+            lse_src[r, b, t : t + 1, :] = m + jnp.log2(s)
+
+    def join(parts):
+        m = jnp.max(parts, axis=0)
+        return m + jnp.log2(jnp.sum(jnp.exp2(parts - m[None]), axis=0))
 
     def row_update(r):
-        def some_tiles(step, carry):
-            ids = [lax.rem(code + 1 + step * group + u, n_code) for u in range(group)]
-            for d in ids:
-                x = cells[d] + col_b[place(d // block_tiles)]
-                x = x.reshape(size // SUB, SUB, LANES)
-                m8 = jnp.max(x, axis=0)
-                s8 = jnp.sum(jnp.exp2(x - m8[None]), axis=0)
-                m = jnp.max(m8, axis=0, keepdims=True)
-                s = jnp.sum(s8 * jnp.exp2(m8 - m), axis=0, keepdims=True)
-                lse_src[r, d] = m + jnp.log2(s)
-            for u, d in enumerate(ids):
-
-                @pl.when(step * group + u < n_code - 1)
-                def _():
-                    remote(
-                        lse_src.at[r, d], lse_in.at[r, code], lse_send.at[r], lse_recv.at[r], dp, d
-                    ).start()
-
-            return carry
-
-        lax.fori_loop(0, tiles // group, some_tiles, 0)
-        lse_in[r, code] = lse_src[r, code]
-        some = pl.ds(0, n_code - 1)
-        all_in = remote(
-            lse_src.at[r, some], lse_in.at[r, some], lse_send.at[r], lse_recv.at[r], dp, code
-        )
-        all_in.wait_recv()
-        parts = lse_in[r]
-        m = jnp.max(parts, axis=0)
-        s = jnp.sum(jnp.exp2(parts - m[None]), axis=0)
-        value = -(m + jnp.log2(s))
-        row_src[r] = value
-        row_in[r, code] = value
-
-        def tell(j, carry):
-            to = lax.rem(code + 1 + j, n_code)
+        def one_block(step, carry):
+            b = lax.rem(share + 1 + step, shares)
+            row_block(r, b)
             remote(
-                row_src.at[r], row_in.at[r, code], row_send.at[r], row_recv.at[r], dp, to
+                lse_src.at[r, b],
+                lse_in.at[r, share],
+                lse_send.at[r],
+                lse_recv.at[r],
+                dp,
+                mate(b),
             ).start()
             return carry
 
-        lax.fori_loop(0, n_code - 1, tell, 0)
-        all_in.wait_send()
-        all_rows = remote(
-            lse_src.at[r, some], row_in.at[r, some], row_send.at[r], row_recv.at[r], dp, code
-        )
-        all_rows.wait_recv()
-        row_b[...] = jnp.broadcast_to(row_in[r], row_b.shape)
-        all_rows.wait_send()
+        lax.fori_loop(0, shares - 1, one_block, 0)
+        row_block(r, share)
+        lse_in[r, share] = lse_src[r, share]
+        others = pl.ds(0, shares - 1)
+        first = remote(
+            lse_src.at[r, others], lse_in.at[r, others], lse_send.at[r], lse_recv.at[r], dp, code
+        )
+        first.wait_recv()
+        value = join(lse_in[r])
+        mid_src[r] = value
+        for step in range(1, quarters):
+            remote(
+                mid_src.at[r],
+                mid_in.at[r, quarter],
+                mid_send.at[r],
+                mid_recv.at[r],
+                dp,
+                far_mate((quarter + step) % quarters),
+            ).start()
+        mid_in[r, quarter] = value
+        some = pl.ds(0, quarters - 1)
+        second = remote(
+            mid_in.at[r, some], mid_in.at[r, some], mid_send.at[r], mid_recv.at[r], dp, code
+        )
+        second.wait_recv()
+        value = -join(mid_in[r])
+        row_src[r] = value
+        for step in range(1, shares):
+            remote(
+                row_src.at[r],
+                row_in.at[r, share],
+                row_send.at[r],
+                row_recv.at[r],
+                dp,
+                mate((share + step) % shares),
+            ).start()
+        row_in[r, share] = value
+        first.wait_send()
+        second.wait_send()
+        third = remote(
+            row_in.at[r, others], row_in.at[r, others], row_send.at[r], row_recv.at[r], dp, code
+        )
+        third.wait_recv()
+        for b in range(blocks):
+            for t in range(block_tiles):
+                row_b[b * block_tiles + t] = jnp.broadcast_to(
+                    row_in[r, b, t : t + 1, :], (SUB, LANES)
+                )
+        third.wait_send()
 
     def col_update(r, target):
         def some_cols(j, carry):
@@ -377,24 +420,34 @@
         ).wait_recv()
     for copy in mass_copies:
         copy.wait_send()
-    mass_all = mass_in[0, 0] + mass_src[1] + mass_in[1, 0]
-    mass_ref[...] = mass_all
-    for h in range(halves):
-        peak[0, h * LANES : (h + 1) * LANES, :] = to_column(mass_all[h : h + 1])
+    mass_ref[...] = mass_in[0, 0] + mass_src[1] + mass_in[1, 0]
 
     def finish(n, carry):
         for s in range(2):
             remote(
                 num_src.at[s, n], num_in.at[s, n], num_send.at[s, n], num_recv.at[s, n], dp, code
             ).wait()
-        whole = (
+        whole_ref[n] = (
             num_in[0, n].astype(jnp.float32) + num_own[n] + num_in[1, n].astype(jnp.float32)
         )
-        divisor = jnp.concatenate([peak[0]] * (piece // LANES), axis=1)
-        out_ref[:, columns(n)] = (whole / divisor).astype(jnp.bfloat16)
         return carry
 
     lax.fori_loop(0, PIECES, finish, 0)
+
+
+def divide(whole_ref, mass_in_ref, out_ref, mass_ref):
+    size, piece = whole_ref.shape[1], whole_ref.shape[2]
+    eye = lax.broadcasted_iota(jnp.int32, (LANES, LANES), 0) == lax.broadcasted_iota(
+        jnp.int32, (LANES, LANES), 1
+    )
+    mass_ref[...] = mass_in_ref[...]
+    for h in range(size // LANES):
+        row = jnp.broadcast_to(mass_in_ref[h : h + 1, :], (LANES, LANES))
+        column = jnp.sum(jnp.where(eye, row, 0.0), axis=1, keepdims=True)
+        span = slice(h * LANES, (h + 1) * LANES)
+        for n in range(PIECES):
+            value = whole_ref[n, span, :] / column
+            out_ref[span, n * piece : (n + 1) * piece] = value.astype(out_ref.dtype)
 
 
 def solution(mesh):
@@ -404,15 +457,17 @@
         rows, width = features.shape
         size = centroids.shape[0]
         tiles = rows // LANES
+        blocks = block_lists.shape[0]
+        block_tiles = tiles // blocks
         halves = size // LANES
         piece = width // PIECES
         updates = ROUNDS + 1
         f32, bf16 = jnp.float32, jnp.bfloat16
         dma = pltpu.SemaphoreType.DMA
-        new_centroids, mass = pl.pallas_call(
+        whole, mass = pl.pallas_call(
             functools.partial(kernel, n_dp, n_code),
             out_shape=(
-                jax.ShapeDtypeStruct((size, width), bf16),
+                jax.ShapeDtypeStruct((PIECES, size, piece), f32),
                 jax.ShapeDtypeStruct((halves, LANES), f32),
             ),
             in_specs=[
@@ -433,10 +488,12 @@
                 pltpu.VMEM((3, size, LANES), f32),
                 pltpu.VMEM((3, size, LANES), f32),
                 pltpu.VMEM((3, size, rows), bf16),
-                pltpu.VMEM((updates, tiles, 1, LANES), f32),
-                pltpu.VMEM((updates, tiles, 1, LANES), f32),
-                pltpu.VMEM((updates, 1, LANES), f32),
-                pltpu.VMEM((updates, tiles, 1, LANES), f32),
+                pltpu.VMEM((updates, blocks, block_tiles, LANES), f32),
+                pltpu.VMEM((updates, blocks, block_tiles, LANES), f32),
+                pltpu.VMEM((updates, block_tiles, LANES), f32),
+                pltpu.VMEM((updates, Z // NEAR, block_tiles, LANES), f32),
+                pltpu.VMEM((updates, block_tiles, LANES), f32),
+                pltpu.VMEM((updates, blocks, block_tiles, LANES), f32),
                 pltpu.VMEM((ROUNDS, 3, halves, LANES), f32),
                 pltpu.VMEM((ROUNDS, 1, halves, LANES), f32),
                 pltpu.VMEM((ROUNDS, 2, halves, LANES), f32),
@@ -447,10 +504,12 @@
                 pltpu.VMEM((2, PIECES, size, piece), bf16),
                 pltpu.VMEM((2, PIECES, size, piece), bf16),
                 pltpu.VMEM((PIECES, size, piece), f32),
-                dma((block_lists.shape[0],)),
+                dma((blocks,)),
                 dma,
                 dma((2,)),
                 dma((2,)),
+                dma((updates,)),
+                dma((updates,)),
                 dma((updates,)),
                 dma((updates,)),
                 dma((updates,)),
@@ -472,6 +531,17 @@
             ),
             name="balanced_kmeans",
         )(block_lists, features, centroids)
+        new_centroids, mass = pl.pallas_call(
+            divide,
+            out_shape=(
+                jax.ShapeDtypeStruct((size, width), bf16),
+                jax.ShapeDtypeStruct((halves, LANES), f32),
+            ),
+            cost_estimate=pl.CostEstimate(
+                flops=size * width, bytes_accessed=6 * size * width, transcendentals=0
+            ),
+            name="divide",
+        )(whole, mass)
         return new_centroids, mass.reshape(size)
 
     return jax.shard_map(

time: 133 us -> 130 us (0.977)
  local copies, waits for them, and re-layouts: 2.96 us -> 0 us
    unnamed x2 -> x0, local copies, waits for them, and re-layouts: 2.96 us -> none
    pallas_call x1, Pallas kernels: 129 us -> 127 us  [local(): pl.pallas_call(functools.partial(kernel, n_dp, n_code), out_shape=(jax.Sh...]
    pallas_call x0 -> x1, Pallas kernels: none -> 2.02 us  [local(): pl.pallas_call(divide, out_shape=(jax.ShapeDtypeStruct((size, width), bf1...]
where the time goes in v2:
time: 130 us; the launch traced here: 129 us
  Pallas kernels  129 us (99%)
    pallas_call x1, Pallas kernels, local(): pl.pallas_call(functools.partial(kernel, n_dp, n_code), out_shape=(jax.Sh...  127 us

profile of v2, /device:TPU:1, one launch (start us, length us, event | category | flops | bytes accessed | tf_op | source)
XLA Modules:
  0.0 129.4 jit_solution(9471748195538137739)
XLA Ops:
  0.6 126.8 %balanced_kmeans.1 = (f32[3,256,256]{2,1,0:T(8,128)}, f32[2,128]{1,0:T(2,128)}) custom-call(s32[8,32]{1,0:T(8,128)} %lists_ref.1, bf16[4096,768]{1,0:T(8,128)(2,1)} %feat_hbm.1, bf16[256,768]{1,0:T(8,128)(2,1)} %cent_hbm.1), custom_call_target="tpu_custom_call" | custom-call | flops 6442450944 | bytes 7077888 | tf_op jit(solution)/shard_map/balanced_kmeans/pallas_call | solution.py:467
  127.4 2.0 %divide.1 = (bf16[256,768]{1,0:T(8,128)(2,1)}, f32[2,128]{1,0:T(2,128)}) custom-call(f32[3,256,256]{2,1,0:T(8,128)} %get-tuple-element.6.whole_ref, f32[2,128]{1,0:T(2,128)} %get-tuple-element.7.mass_in_ref), custom_call_target="tpu_custom_call" | custom-call | flops 196608 | bytes 1179648 | tf_op jit(solution)/shard_map/divide/pallas_call | solution.py:534

commit v3 on v2

--- a/solution.py
+++ b/solution.py
@@ -36,6 +36,7 @@
     peak,
     total,
     weight,
+    places,
     lse_src,
     lse_in,
     mid_src,
@@ -51,7 +52,7 @@
     mass_in,
     num_src,
     num_in,
-    num_own,
+    num_sum,
     feat_sem,
     own_sem,
     halo_send,
@@ -80,23 +81,22 @@
     halves = size // LANES
     piece = width // PIECES
     odd = lax.rem(dp, 2)
-
-    y_hi, z = code // Z, lax.rem(code, Z)
-    quarter, near = z // NEAR, lax.rem(z, NEAR)
+    dp_near = {step: lax.rem(dp + (n_dp + step), n_dp) for step in (-2, -1, 1, 2)}
+    for b in range(blocks):
+        places[b] = jnp.minimum(lax.rem(lists_ref[b, code] + (n_dp + 1) - dp, n_dp), 2)
+
+    y_hi, z = lax.div(code, Z), lax.rem(code, Z)
+    quarter, near = lax.div(z, NEAR), lax.rem(z, NEAR)
     quarters, shares = Z // NEAR, NEAR * (n_code // Z)
     share = y_hi * NEAR + near
-
-    def mate(other):
-        return (other // NEAR) * Z + quarter * NEAR + lax.rem(other, NEAR)
-
-    def far_mate(other):
-        return y_hi * Z + other * NEAR + near
-
-    def dp_at(step):
-        return lax.rem(dp + (n_dp + step), n_dp)
-
-    def place(b):
-        return jnp.minimum(lax.rem(lists_ref[b, code] + (n_dp + 1) - dp, n_dp), 2)
+    mates = []
+    for step in range(1, shares):
+        other = lax.rem(share + step, shares)
+        at = lax.div(other, NEAR) * Z + quarter * NEAR + lax.rem(other, NEAR)
+        mates.append((other, at))
+    far_mates = []
+    for step in range(1, quarters):
+        far_mates.append(y_hi * Z + lax.rem(quarter + step, quarters) * NEAR + near)
 
     def feat_copy(b):
         span = pl.ds(b * block_rows, block_rows)
@@ -120,29 +120,19 @@
     barrier = pltpu.get_barrier_semaphore()
     for step in (-1, 1, -2, 2):
         pl.semaphore_signal(
-            barrier, inc=1, device_id=(dp_at(step), code), device_id_type=MESH
-        )
-    for step in range(1, shares):
-        pl.semaphore_signal(
-            barrier, inc=1, device_id=(dp, mate((share + step) % shares)), device_id_type=MESH
-        )
-    for step in range(1, quarters):
-        to = far_mate((quarter + step) % quarters)
+            barrier, inc=1, device_id=(dp_near[step], code), device_id_type=MESH
+        )
+    for to in [at for _, at in mates] + far_mates:
         pl.semaphore_signal(barrier, inc=1, device_id=(dp, to), device_id_type=MESH)
     pl.semaphore_wait(barrier, 4 + shares - 1 + quarters - 1)
 
-    def side(s):
-        return 2 * lax.rem(odd + s, 2)
+    ups = (odd, 1 - odd)
+    sides = [dp_near[-1] + up * (dp_near[1] - dp_near[-1]) for up in ups]
 
     def halo(s):
-        w = side(s)
+        land = 1 - ups[s]
         return remote(
-            cent_hbm,
-            win.at[2 - w],
-            halo_send.at[s],
-            halo_recv.at[1 - w // 2],
-            dp_at(w - 1),
-            code,
+            cent_hbm, win.at[2 * land], halo_send.at[s], halo_recv.at[land], sides[s], code
         )
 
     halo(0).start()
@@ -176,7 +166,7 @@
     def score(b, carry):
         feat_copy(b).wait()
         inner = lax.dot_general(
-            win[place(b)],
+            win[places[b]],
             feat[pl.ds(pl.multiple_of(b * block_rows, block_rows), block_rows), :],
             (((1,), (1,)), ((), ())),
             preferred_element_type=jnp.float32,
@@ -191,7 +181,7 @@
     norms(2)
 
     def row_block(r, b):
-        bias = col_b[place(b)]
+        bias = col_b[places[b]]
         for t in range(block_tiles):
             x = (cells[b * block_tiles + t] + bias).reshape(size // SUB, SUB, LANES)
             m8 = jnp.max(x, axis=0)
@@ -205,21 +195,16 @@
         return m + jnp.log2(jnp.sum(jnp.exp2(parts - m[None]), axis=0))
 
     def row_update(r):
-        def one_block(step, carry):
-            b = lax.rem(share + 1 + step, shares)
-            row_block(r, b)
+        def two_blocks(step, carry):
+            row_block(r, 2 * step)
+            row_block(r, 2 * step + 1)
+            return carry
+
+        lax.fori_loop(0, blocks // 2, two_blocks, 0)
+        for b, to in mates:
             remote(
-                lse_src.at[r, b],
-                lse_in.at[r, share],
-                lse_send.at[r],
-                lse_recv.at[r],
-                dp,
-                mate(b),
+                lse_src.at[r, b], lse_in.at[r, share], lse_send.at[r], lse_recv.at[r], dp, to
             ).start()
-            return carry
-
-        lax.fori_loop(0, shares - 1, one_block, 0)
-        row_block(r, share)
         lse_in[r, share] = lse_src[r, share]
         others = pl.ds(0, shares - 1)
         first = remote(
@@ -228,14 +213,9 @@
         first.wait_recv()
         value = join(lse_in[r])
         mid_src[r] = value
-        for step in range(1, quarters):
+        for to in far_mates:
             remote(
-                mid_src.at[r],
-                mid_in.at[r, quarter],
-                mid_send.at[r],
-                mid_recv.at[r],
-                dp,
-                far_mate((quarter + step) % quarters),
+                mid_src.at[r], mid_in.at[r, quarter], mid_send.at[r], mid_recv.at[r], dp, to
             ).start()
         mid_in[r, quarter] = value
         some = pl.ds(0, quarters - 1)
@@ -245,14 +225,9 @@
         second.wait_recv()
         value = -join(mid_in[r])
         row_src[r] = value
-        for step in range(1, shares):
+        for _, to in mates:
             remote(
-                row_src.at[r],
-                row_in.at[r, share],
-                row_send.at[r],
-                row_recv.at[r],
-                dp,
-                mate((share + step) % shares),
+                row_src.at[r], row_in.at[r, share], row_send.at[r], row_recv.at[r], dp, to
             ).start()
         row_in[r, share] = value
         first.wait_send()
@@ -269,29 +244,31 @@
         third.wait_send()
 
     def col_update(r, target):
-        def some_cols(j, carry):
+        def one_tile(j):
             span = pl.ds(pl.multiple_of(j * SUB, SUB), SUB)
             x = cells[:, span, :] + row_b[...]
             x = x.reshape(blocks, block_tiles, SUB, LANES)
-            places = [jnp.full((SUB, LANES), place(b), jnp.int32) for b in range(blocks)]
+            at = [jnp.full((SUB, LANES), places[b], jnp.int32) for b in range(blocks)]
             tops = [jnp.max(x[b], axis=0) for b in range(blocks)]
             peaks = []
             for w in range(3):
-                held = [jnp.where(places[b] == w, tops[b], LOWEST) for b in range(blocks)]
+                held = [jnp.where(at[b] == w, tops[b], LOWEST) for b in range(blocks)]
                 peaks.append(functools.reduce(jnp.maximum, held))
             sums = []
             for b in range(blocks):
-                top = jnp.where(
-                    places[b] == 0, peaks[0], jnp.where(places[b] == 1, peaks[1], peaks[2])
-                )
+                top = jnp.where(at[b] == 0, peaks[0], jnp.where(at[b] == 1, peaks[1], peaks[2]))
                 sums.append(jnp.sum(jnp.exp2(x[b] - top[None]), axis=0))
             for w in range(3):
-                held = [jnp.where(places[b] == w, sums[b], 0.0) for b in range(blocks)]
+                held = [jnp.where(at[b] == w, sums[b], 0.0) for b in range(blocks)]
                 peak[w, span, :] = peaks[w]
                 total[w, span, :] = functools.reduce(jnp.add, held)
+
+        def two_tiles(j, carry):
+            one_tile(2 * j)
+            one_tile(2 * j + 1)
             return carry
 
-        lax.fori_loop(0, size // SUB, some_cols, 0)
+        lax.fori_loop(0, size // SUB // 2, two_tiles, 0)
         m = jnp.max(peak[...], axis=2, keepdims=True)
         s = jnp.sum(total[...] * jnp.exp2(peak[...] - m), axis=2, keepdims=True)
         mine = to_lanes(jnp.broadcast_to(m, peak.shape)) + jnp.log2(
@@ -304,7 +281,7 @@
                 there.at[r],
                 col_send.at[r, slot],
                 col_recv.at[r, slot],
-                dp_at(step),
+                dp_near[step],
                 code,
             )
             for slot, (step, start, count, there) in enumerate(
@@ -346,20 +323,18 @@
         span = pl.ds(pl.multiple_of(j * pack, pack), pack)
         sums = [jnp.zeros((2, SUB, LANES), jnp.float32) for w in range(3)]
         for b in range(blocks):
-            at = place(b)
-            at_b = jnp.full((2, SUB, LANES), at, jnp.int32)
-            g = col_b[at, span, :].reshape(2, SUB, LANES)
+            g = col_b[places[b], span, :].reshape(2, SUB, LANES)
             here = jnp.zeros((2, SUB, LANES), jnp.float32)
             for t in range(block_tiles):
                 d = b * block_tiles + t
                 x = cells[d, span, :].reshape(2, SUB, LANES) + row_b[d][None] + g
                 value = jnp.exp2(x)
                 here = here + value
-                for w in range(3):
-                    kept = jnp.where(at_b == w, value, 0.0).reshape(pack, LANES)
-                    weight[w, span, d * LANES : (d + 1) * LANES] = kept.astype(jnp.bfloat16)
+                low = value.reshape(pack, LANES).astype(jnp.bfloat16)
+                weight[b, span, t * LANES : (t + 1) * LANES] = low
+            at = jnp.full((2, SUB, LANES), places[b], jnp.int32)
             for w in range(3):
-                sums[w] = sums[w] + jnp.where(at_b == w, here, 0.0)
+                sums[w] = sums[w] + jnp.where(at == w, here, 0.0)
         for w in range(3):
             total[w, span, :] = sums[w].reshape(pack, LANES)
         return carry
@@ -375,7 +350,7 @@
             mass_in.at[1 - s],
             mass_send.at[s],
             mass_recv.at[1 - s],
-            dp_at(2 * s - 1),
+            dp_near[2 * s - 1],
             code,
         )
         for s in range(2)
@@ -386,33 +361,41 @@
     def columns(n):
         return pl.ds(pl.multiple_of(n * piece, piece), piece)
 
-    def numerator(w, n):
-        return jnp.dot(weight[w], feat[:, columns(n)], preferred_element_type=jnp.float32)
-
     def num_copy(s, n):
-        w = side(s)
+        land = 1 - ups[s]
         return remote(
             num_src.at[s, n],
-            num_in.at[1 - w // 2, n],
+            num_in.at[land, n],
             num_send.at[s, n],
-            num_recv.at[1 - w // 2, n],
-            dp_at(w - 1),
+            num_recv.at[land, n],
+            sides[s],
             code,
         )
 
-    def give(q, carry):
-        s, n = q // PIECES, lax.rem(q, PIECES)
-        num_src[s, n] = numerator(side(s), n).astype(jnp.bfloat16)
-        num_copy(s, n).start()
+    def numerators(n, carry):
+        for w in range(3):
+            num_sum[n, w] = jnp.zeros((size, piece), jnp.float32)
+
+        def two_blocks(step, carry):
+            products = []
+            for b in (2 * step, 2 * step + 1):
+                span = pl.ds(pl.multiple_of(b * block_rows, block_rows), block_rows)
+                product = jnp.dot(
+                    weight[b], feat[span, columns(n)], preferred_element_type=jnp.float32
+                )
+                products.append((jnp.full(product.shape, places[b], jnp.int32), product))
+            for w in range(3):
+                held = [jnp.where(at == w, product, 0.0) for at, product in products]
+                num_sum[n, w] = num_sum[n, w] + (held[0] + held[1])
+            return carry
+
+        lax.fori_loop(0, blocks // 2, two_blocks, 0)
+        for s in range(2):
+            num_src[s, n] = num_sum[n, 2 * ups[s]].astype(jnp.bfloat16)
+            num_copy(s, n).start()
         return carry
 
-    lax.fori_loop(0, 2 * PIECES, give, 0)
-
-    def keep(n, carry):
-        num_own[n] = numerator(1, n).astype(jnp.bfloat16).astype(jnp.float32)
-        return carry
-
-    lax.fori_loop(0, PIECES, keep, 0)
+    lax.fori_loop(0, PIECES, numerators, 0)
 
     for s in range(2):
         remote(
@@ -427,8 +410,9 @@
             remote(
                 num_src.at[s, n], num_in.at[s, n], num_send.at[s, n], num_recv.at[s, n], dp, code
             ).wait()
+        own = num_sum[n, 1].astype(jnp.bfloat16).astype(jnp.float32)
         whole_ref[n] = (
-            num_in[0, n].astype(jnp.float32) + num_own[n] + num_in[1, n].astype(jnp.float32)
+            num_in[0, n].astype(jnp.float32) + own + num_in[1, n].astype(jnp.float32)
         )
         return carry
 
@@ -487,7 +471,8 @@
                 pltpu.VMEM((3, size, LANES), f32),
                 pltpu.VMEM((3, size, LANES), f32),
                 pltpu.VMEM((3, size, LANES), f32),
-                pltpu.VMEM((3, size, rows), bf16),
+                pltpu.VMEM((blocks, size, rows // blocks), bf16),
+                pltpu.SMEM((blocks,), jnp.int32),
                 pltpu.VMEM((updates, blocks, block_tiles, LANES), f32),
                 pltpu.VMEM((updates, blocks, block_tiles, LANES), f32),
                 pltpu.VMEM((updates, block_tiles, LANES), f32),
@@ -503,7 +488,7 @@
                 pltpu.VMEM((2, 1, halves, LANES), f32),
                 pltpu.VMEM((2, PIECES, size, piece), bf16),
                 pltpu.VMEM((2, PIECES, size, piece), bf16),
-                pltpu.VMEM((PIECES, size, piece), f32),
+                pltpu.VMEM((PIECES, 3, size, piece), f32),
                 dma((blocks,)),
                 dma,
                 dma((2,)),

time: 130 us -> 129 us (level)
  no operation moved by 1% of the time
where the time goes in v3:
time: 129 us
  Pallas kernels  128 us (99%)
    pallas_call x1, Pallas kernels, local(): pl.pallas_call(functools.partial(kernel, n_dp, n_code), out_shape=(jax.Sh...  126 us

profile of v3, /device:TPU:1, one launch (start us, length us, event | category | flops | bytes accessed | tf_op | source)
XLA Modules:
  0.0 128.8 jit_solution(17299849056634138634)
XLA Ops:
  0.6 126.1 %balanced_kmeans.1 = (f32[3,256,256]{2,1,0:T(8,128)}, f32[2,128]{1,0:T(2,128)}) custom-call(s32[8,32]{1,0:T(8,128)} %lists_ref.1, bf16[4096,768]{1,0:T(8,128)(2,1)} %feat_hbm.1, bf16[256,768]{1,0:T(8,128)(2,1)} %cent_hbm.1), custom_call_target="tpu_custom_call" | custom-call | flops 6442450944 | bytes 7077888 | tf_op jit(solution)/shard_map/balanced_kmeans/pallas_call | solution.py:451
  126.8 2.0 %divide.1 = (bf16[256,768]{1,0:T(8,128)(2,1)}, f32[2,128]{1,0:T(2,128)}) custom-call(f32[3,256,256]{2,1,0:T(8,128)} %get-tuple-element.6.whole_ref, f32[2,128]{1,0:T(2,128)} %get-tuple-element.7.mass_in_ref), custom_call_target="tpu_custom_call" | custom-call | flops 196608 | bytes 1179648 | tf_op jit(solution)/shard_map/divide/pallas_call | solution.py:519

commit v4 on v3

v4 whole, which is shorter than its diff:
```python
import functools
import math

import jax
import jax.numpy as jnp
from jax import lax
from jax.experimental import pallas as pl
from jax.experimental.pallas import tpu as pltpu
from jax.sharding import PartitionSpec as P

ROUNDS = 3
SOFTMAX_TEMP = 12.0
LOG2E = math.log2(math.e)
LOWEST = -3.0e38
LANES = 128
SUB = 8
PIECES = 3
Z = 16
NEAR = 4
MESH = pl.DeviceIdType.MESH


def remote(src, dst, send, recv, to_dp, to_code):
    return pltpu.make_async_remote_copy(
        src_ref=src,
        dst_ref=dst,
        send_sem=send,
        recv_sem=recv,
        device_id=(to_dp, to_code),
        device_id_type=MESH,
    )


def sides_of(n_dp):
    dp = lax.axis_index("dp")
    odd = lax.rem(dp, 2)
    left, right = lax.rem(dp + n_dp - 1, n_dp), lax.rem(dp + 1, n_dp)
    ups = (odd, 1 - odd)
    return ups, [left + up * (right - left) for up in ups]


def greet(partners):
    barrier = pltpu.get_barrier_semaphore()
    for to in partners:
        pl.semaphore_signal(barrier, inc=1, device_id=to, device_id_type=MESH)
    pl.semaphore_wait(barrier, len(partners))


def read_places(n_dp, lists_ref, places):
    dp, code = lax.axis_index("dp"), lax.axis_index("code")
    for b in range(lists_ref.shape[0]):
        places[b] = jnp.minimum(lax.rem(lists_ref[b, code] + (n_dp + 1) - dp, n_dp), 2)


def halo_kernel(n_dp, cent_hbm, win_ref, win, own_sem, send, recv):
    dp, code = lax.axis_index("dp"), lax.axis_index("code")
    own = pltpu.make_async_copy(cent_hbm, win.at[1], own_sem)
    own.start()
    ups, sides = sides_of(n_dp)
    greet([(to, code) for to in sides])
    copies = []
    for s in range(2):
        land = 1 - ups[s]
        copies.append(
            remote(cent_hbm, win.at[2 * land], send.at[s], recv.at[land], sides[s], code)
        )
    for copy in copies:
        copy.start()
    own.wait()
    win_ref[1] = win[1]
    for copy in copies:
        copy.wait_send()
    for s in range(2):
        remote(cent_hbm, win.at[2 * s], send.at[s], recv.at[s], dp, code).wait_recv()
    win_ref[0] = win[0]
    win_ref[2] = win[2]


def score_kernel(n_dp, lists_ref, win_ref, feat_ref, inner_ref, bias_ref, places):
    b = pl.program_id(0)

    @pl.when(b == 0)
    def _():
        read_places(n_dp, lists_ref, places)
        for w in range(3):
            wide = win_ref[w].astype(jnp.float32)
            norm = jnp.sum(wide * wide, axis=1, keepdims=True)
            bias_ref[w] = jnp.broadcast_to(norm * (-LOG2E / SOFTMAX_TEMP), bias_ref.shape[1:])

    inner = lax.dot_general(
        win_ref[places[b]],
        feat_ref[...],
        (((1,), (1,)), ((), ())),
        preferred_element_type=jnp.float32,
    )
    inner_ref[0] = inner.astype(jnp.bfloat16)


def sum_kernel(n_dp, lists_ref, weight_ref, feat_ref, out_ref, total, places):
    b = pl.program_id(0)

    @pl.when(b == 0)
    def _():
        read_places(n_dp, lists_ref, places)
        total[...] = jnp.zeros_like(total)

    w = places[b]
    total[w] = total[w] + jnp.dot(
        weight_ref[0], feat_ref[...], preferred_element_type=jnp.float32
    )

    @pl.when(b == pl.num_programs(0) - 1)
    def _():
        out_ref[...] = total[...].astype(jnp.bfloat16)


def exchange_kernel(n_dp, num_ref, mass_ref, whole_ref, mass_out, num_in, mass_in, send, recv, m_send, m_recv):
    dp, code = lax.axis_index("dp"), lax.axis_index("code")
    ups, sides = sides_of(n_dp)
    greet([(to, code) for to in sides])
    copies = []
    for s in range(2):
        land = 1 - ups[s]
        copies.append(
            remote(
                mass_ref.at[2 * ups[s]], mass_in.at[land], m_send.at[s], m_recv.at[land], sides[s], code
            )
        )
        copies.append(
            remote(num_ref.at[2 * ups[s]], num_in.at[land], send.at[s], recv.at[land], sides[s], code)
        )
    for copy in copies:
        copy.start()
    for copy in copies:
        copy.wait_send()
    for s in range(2):
        remote(mass_ref.at[0], mass_in.at[s], m_send.at[s], m_recv.at[s], dp, code).wait_recv()
        remote(num_ref.at[0], num_in.at[s], send.at[s], recv.at[s], dp, code).wait_recv()
    mass_out[...] = mass_in[0] + mass_ref[1] + mass_in[1]
    whole_ref[...] = (
        num_in[0].astype(jnp.float32)
        + num_ref[1].astype(jnp.float32)
        + num_in[1].astype(jnp.float32)
    )


def scale_kernel(
    n_dp,
    n_code,
    lists_ref,
    inner_ref,
    bias_ref,
    weight,
    mass_ref,
    cells,
    row_b,
    col_b,
    peak,
    total,
    places,
    lse_src,
    lse_in,
    mid_src,
    mid_in,
    row_src,
    row_in,
    col_src,
    col_l2,
    col_l1,
    col_r1,
    col_r2,
    lse_send,
    lse_recv,
    mid_send,
    mid_recv,
    row_send,
    row_recv,
    col_send,
    col_recv,
):
    dp = lax.axis_index("dp")
    code = lax.axis_index("code")
    blocks = lists_ref.shape[0]
    size, block_rows = inner_ref.shape[1], inner_ref.shape[2]
    rows = blocks * block_rows
    block_tiles = block_rows // LANES
    halves = size // LANES
    dp_near = {step: lax.rem(dp + (n_dp + step), n_dp) for step in (-2, -1, 1, 2)}
    read_places(n_dp, lists_ref, places)

    y_hi, z = lax.div(code, Z), lax.rem(code, Z)
    quarter, near = lax.div(z, NEAR), lax.rem(z, NEAR)
    quarters, shares = Z // NEAR, NEAR * (n_code // Z)
    share = y_hi * NEAR + near
    mates = []
    for step in range(1, shares):
        other = lax.rem(share + step, shares)
        at = lax.div(other, NEAR) * Z + quarter * NEAR + lax.rem(other, NEAR)
        mates.append((other, at))
    far_mates = []
    for step in range(1, quarters):
        far_mates.append(y_hi * Z + lax.rem(quarter + step, quarters) * NEAR + near)

    greet(
        [(dp_near[step], code) for step in (-1, 1, -2, 2)]
        + [(dp, at) for _, at in mates]
        + [(dp, at) for at in far_mates]
    )
    col_b[...] = bias_ref[...]

    def unfold(b, carry):
        scaled = inner_ref[b].astype(jnp.float32) * (2.0 * LOG2E / SOFTMAX_TEMP)
        for t in range(block_tiles):
            cells[b * block_tiles + t] = scaled[:, t * LANES : (t + 1) * LANES]
        return carry

    lax.fori_loop(0, blocks, unfold, 0)

    eye = lax.broadcasted_iota(jnp.int32, (LANES, LANES), 0) == lax.broadcasted_iota(
        jnp.int32, (LANES, LANES), 1
    )

    def to_lanes(column):
        square = column.reshape(3 * halves, LANES, LANES)
        flat = jnp.sum(jnp.where(eye[None], square, 0.0), axis=1)
        return flat.reshape(3, halves, LANES)

    def to_column(row):
        square = jnp.where(eye, jnp.broadcast_to(row, (LANES, LANES)), 0.0)
        return jnp.broadcast_to(jnp.sum(square, axis=1, keepdims=True), (LANES, LANES))

    def row_block(r, b):
        bias = col_b[places[b]]
        for t in range(block_tiles):
            x = (cells[b * block_tiles + t] + bias).reshape(size // SUB, SUB, LANES)
            m8 = jnp.max(x, axis=0)
            s8 = jnp.sum(jnp.exp2(x - m8[None]), axis=0)
            m = jnp.max(m8, axis=0, keepdims=True)
            s = jnp.sum(s8 * jnp.exp2(m8 - m), axis=0, keepdims=True)
            lse_src[r, b, t : t + 1, :] = m + jnp.log2(s)

    def join(parts):
        m = jnp.max(parts, axis=0)
        return m + jnp.log2(jnp.sum(jnp.exp2(parts - m[None]), axis=0))

    def row_update(r):
        def two_blocks(step, carry):
            row_block(r, 2 * step)
            row_block(r, 2 * step + 1)
            return carry

        lax.fori_loop(0, blocks // 2, two_blocks, 0)
        for b, to in mates:
            remote(
                lse_src.at[r, b], lse_in.at[r, share], lse_send.at[r], lse_recv.at[r], dp, to
            ).start()
        lse_in[r, share] = lse_src[r, share]
        others = pl.ds(0, shares - 1)
        first = remote(
            lse_src.at[r, others], lse_in.at[r, others], lse_send.at[r], lse_recv.at[r], dp, code
        )
        first.wait_recv()
        value = join(lse_in[r])
        mid_src[r] = value
        for to in far_mates:
            remote(
                mid_src.at[r], mid_in.at[r, quarter], mid_send.at[r], mid_recv.at[r], dp, to
            ).start()
        mid_in[r, quarter] = value
        some = pl.ds(0, quarters - 1)
        second = remote(
            mid_in.at[r, some], mid_in.at[r, some], mid_send.at[r], mid_recv.at[r], dp, code
        )
        second.wait_recv()
        value = -join(mid_in[r])
        row_src[r] = value
        for _, to in mates:
            remote(
                row_src.at[r], row_in.at[r, share], row_send.at[r], row_recv.at[r], dp, to
            ).start()
        row_in[r, share] = value
        first.wait_send()
        second.wait_send()
        third = remote(
            row_in.at[r, others], row_in.at[r, others], row_send.at[r], row_recv.at[r], dp, code
        )
        third.wait_recv()
        for b in range(blocks):
            for t in range(block_tiles):
                row_b[b * block_tiles + t] = jnp.broadcast_to(
                    row_in[r, b, t : t + 1, :], (SUB, LANES)
                )
        third.wait_send()

    def col_update(r, target):
        def one_tile(j):
            span = pl.ds(pl.multiple_of(j * SUB, SUB), SUB)
            x = cells[:, span, :] + row_b[...]
            x = x.reshape(blocks, block_tiles, SUB, LANES)
            at = [jnp.full((SUB, LANES), places[b], jnp.int32) for b in range(blocks)]
            tops = [jnp.max(x[b], axis=0) for b in range(blocks)]
            peaks = []
            for w in range(3):
                held = [jnp.where(at[b] == w, tops[b], LOWEST) for b in range(blocks)]
                peaks.append(functools.reduce(jnp.maximum, held))
            sums = []
            for b in range(blocks):
                top = jnp.where(at[b] == 0, peaks[0], jnp.where(at[b] == 1, peaks[1], peaks[2]))
                sums.append(jnp.sum(jnp.exp2(x[b] - top[None]), axis=0))
            for w in range(3):
                held = [jnp.where(at[b] == w, sums[b], 0.0) for b in range(blocks)]
                peak[w, span, :] = peaks[w]
                total[w, span, :] = functools.reduce(jnp.add, held)

        def two_tiles(j, carry):
            one_tile(2 * j)
            one_tile(2 * j + 1)
            return carry

        lax.fori_loop(0, size // SUB // 2, two_tiles, 0)
        m = jnp.max(peak[...], axis=2, keepdims=True)
        s = jnp.sum(total[...] * jnp.exp2(peak[...] - m), axis=2, keepdims=True)
        mine = to_lanes(jnp.broadcast_to(m, peak.shape)) + jnp.log2(
            to_lanes(jnp.broadcast_to(s, total.shape))
        )
        col_src[r] = mine
        copies = [
            remote(
                col_src.at[r, pl.ds(start, count)],
                there.at[r],
                col_send.at[r, slot],
                col_recv.at[r, slot],
                dp_near[step],
                code,
            )
            for slot, (step, start, count, there) in enumerate(
                ((-2, 0, 1, col_r2), (2, 2, 1, col_l2), (-1, 0, 2, col_r1), (1, 1, 2, col_l1))
            )
        ]
        for copy in copies:
            copy.start()
        for copy in copies:
            copy.wait_recv()
        l1, r1 = col_l1[r], col_r1[r]
        sets = (
            (col_l2[r, 0], l1[0], mine[0]),
            (l1[1], mine[1], r1[0]),
            (mine[2], r1[1], col_r2[r, 0]),
        )
        for w, terms in enumerate(sets):
            m = functools.reduce(jnp.maximum, terms)
            s = functools.reduce(jnp.add, [jnp.exp2(term - m) for term in terms])
            value = target - (m + jnp.log2(s))
            for h in range(halves):
                col_b[w, h * LANES : (h + 1) * LANES, :] = to_column(value[h : h + 1])
        for copy in copies:
            copy.wait_send()

    target = math.log2((rows * n_dp) / (size * n_dp * n_code))

    def sweep(r, carry):
        row_update(r)
        col_update(r, target)
        return carry

    lax.fori_loop(0, ROUNDS, sweep, 0)
    row_update(ROUNDS)

    pack = 2 * SUB

    def weigh(j, carry):
        span = pl.ds(pl.multiple_of(j * pack, pack), pack)
        sums = [jnp.zeros((2, SUB, LANES), jnp.float32) for w in range(3)]
        for b in range(blocks):
            g = col_b[places[b], span, :].reshape(2, SUB, LANES)
            here = jnp.zeros((2, SUB, LANES), jnp.float32)
            for t in range(block_tiles):
                d = b * block_tiles + t
                x = cells[d, span, :].reshape(2, SUB, LANES) + row_b[d][None] + g
                value = jnp.exp2(x)
                here = here + value
                low = value.reshape(pack, LANES).astype(jnp.bfloat16)
                weight[b, span, t * LANES : (t + 1) * LANES] = low
            at = jnp.full((2, SUB, LANES), places[b], jnp.int32)
            for w in range(3):
                sums[w] = sums[w] + jnp.where(at == w, here, 0.0)
        for w in range(3):
            total[w, span, :] = sums[w].reshape(pack, LANES)
        return carry

    lax.fori_loop(0, size // pack, weigh, 0)

    mass = jnp.sum(total[...], axis=2, keepdims=True)
    mass = to_lanes(jnp.broadcast_to(mass, total.shape))
    mass_ref[...] = mass.astype(jnp.bfloat16).astype(jnp.float32)


def divide(whole_ref, mass_in_ref, out_ref, mass_ref):
    size = whole_ref.shape[0]
    eye = lax.broadcasted_iota(jnp.int32, (LANES, LANES), 0) == lax.broadcasted_iota(
        jnp.int32, (LANES, LANES), 1
    )
    mass_ref[...] = mass_in_ref[...]
    for h in range(size // LANES):
        row = jnp.broadcast_to(mass_in_ref[h : h + 1, :], (LANES, LANES))
        column = jnp.sum(jnp.where(eye, row, 0.0), axis=1, keepdims=True)
        span = slice(h * LANES, (h + 1) * LANES)
        out_ref[span, :] = (whole_ref[span, :] / column).astype(out_ref.dtype)


def solution(mesh):
    n_dp, n_code = mesh.shape["dp"], mesh.shape["code"]

    def local(features, centroids, block_lists):
        rows, width = features.shape
        size = centroids.shape[0]
        tiles = rows // LANES
        blocks = block_lists.shape[0]
        block_rows = rows // blocks
        block_tiles = tiles // blocks
        halves = size // LANES
        updates = ROUNDS + 1
        f32, bf16 = jnp.float32, jnp.bfloat16
        dma = pltpu.SemaphoreType.DMA
        shape = jax.ShapeDtypeStruct
        smem = pl.BlockSpec(memory_space=pltpu.SMEM)
        vmem = pl.BlockSpec(memory_space=pltpu.VMEM)
        anywhere = pl.BlockSpec(memory_space=pl.ANY)
        limit = 48 * 1024 * 1024

        def whole_block(*sizes):
            return pl.BlockSpec(sizes, lambda b: (0,) * len(sizes))

        def per_block(*sizes):
            return pl.BlockSpec(sizes, lambda b: (b,) + (0,) * (len(sizes) - 1))

        window = pl.pallas_call(
            functools.partial(halo_kernel, n_dp),
            out_shape=shape((3, size, width), bf16),
            in_specs=[anywhere],
            out_specs=vmem,
            scratch_shapes=[pltpu.VMEM((3, size, width), bf16), dma, dma((2,)), dma((2,))],
            compiler_params=pltpu.CompilerParams(
                collective_id=0, has_side_effects=True, vmem_limit_bytes=limit
            ),
            name="halo",
        )(centroids)
        inner, bias = pl.pallas_call(
            functools.partial(score_kernel, n_dp),
            grid=(blocks,),
            out_shape=(shape((blocks, size, block_rows), bf16), shape((3, size, LANES), f32)),
            in_specs=[smem, whole_block(3, size, width), per_block(block_rows, width)],
            out_specs=(per_block(1, size, block_rows), whole_block(3, size, LANES)),
            scratch_shapes=[pltpu.SMEM((blocks,), jnp.int32)],
            compiler_params=pltpu.CompilerParams(vmem_limit_bytes=limit),
            name="score",
        )(block_lists, window, features)
        weight, mass = pl.pallas_call(
            functools.partial(scale_kernel, n_dp, n_code),
            out_shape=(shape((blocks, size, block_rows), bf16), shape((3, halves, LANES), f32)),
            in_specs=[smem, vmem, vmem],
            out_specs=(vmem, vmem),
            scratch_shapes=[
                pltpu.VMEM((tiles, size, LANES), f32),
                pltpu.VMEM((tiles, SUB, LANES), f32),
                pltpu.VMEM((3, size, LANES), f32),
                pltpu.VMEM((3, size, LANES), f32),
                pltpu.VMEM((3, size, LANES), f32),
                pltpu.SMEM((blocks,), jnp.int32),
                pltpu.VMEM((updates, blocks, block_tiles, LANES), f32),
                pltpu.VMEM((updates, blocks, block_tiles, LANES), f32),
                pltpu.VMEM((updates, block_tiles, LANES), f32),
                pltpu.VMEM((updates, Z // NEAR, block_tiles, LANES), f32),
                pltpu.VMEM((updates, block_tiles, LANES), f32),
                pltpu.VMEM((updates, blocks, block_tiles, LANES), f32),
                pltpu.VMEM((ROUNDS, 3, halves, LANES), f32),
                pltpu.VMEM((ROUNDS, 1, halves, LANES), f32),
                pltpu.VMEM((ROUNDS, 2, halves, LANES), f32),
                pltpu.VMEM((ROUNDS, 2, halves, LANES), f32),
                pltpu.VMEM((ROUNDS, 1, halves, LANES), f32),
                dma((updates,)),
                dma((updates,)),
                dma((updates,)),
                dma((updates,)),
                dma((updates,)),
                dma((updates,)),
                dma((ROUNDS, 4)),
                dma((ROUNDS, 4)),
            ],
            compiler_params=pltpu.CompilerParams(
                collective_id=1, has_side_effects=True, vmem_limit_bytes=limit
            ),
            name="scale",
        )(block_lists, inner, bias)
        partial_sums = pl.pallas_call(
            functools.partial(sum_kernel, n_dp),
            grid=(blocks,),
            out_shape=shape((3, size, width), bf16),
            in_specs=[smem, per_block(1, size, block_rows), per_block(block_rows, width)],
            out_specs=whole_block(3, size, width),
            scratch_shapes=[pltpu.VMEM((3, size, width), f32), pltpu.SMEM((blocks,), jnp.int32)],
            compiler_params=pltpu.CompilerParams(vmem_limit_bytes=limit),
            name="sums",
        )(block_lists, weight, features)
        whole, mass = pl.pallas_call(
            functools.partial(exchange_kernel, n_dp),
            out_shape=(shape((size, width), f32), shape((halves, LANES), f32)),
            in_specs=[vmem, vmem],
            out_specs=(vmem, vmem),
            scratch_shapes=[
                pltpu.VMEM((2, size, width), bf16),
                pltpu.VMEM((2, halves, LANES), f32),
                dma((2,)),
                dma((2,)),
                dma((2,)),
                dma((2,)),
            ],
            compiler_params=pltpu.CompilerParams(
                collective_id=2, has_side_effects=True, vmem_limit_bytes=limit
            ),
            name="exchange",
        )(partial_sums, mass)
        new_centroids, mass = pl.pallas_call(
            divide,
            out_shape=(shape((size, width), bf16), shape((halves, LANES), f32)),
            name="divide",
        )(whole, mass)
        return new_centroids, mass.reshape(size)

    return jax.shard_map(
        local,
        mesh=mesh,
        in_specs=(P("dp", None), P(("code", "dp"), None), P("dp", None)),
        out_specs=(P(("code", "dp"), None), P(("code", "dp"))),
        check_vma=False,
    )
```

time: 129 us -> 146 us (1.13); the launches traced: 129 us -> 144 us
  Pallas kernels: 128 us -> 140 us
  local copies, waits for them, and re-layouts: 0 us -> 3.14 us
    pallas_call x2 -> x6, Pallas kernels: 128 us -> 140 us  [the longest x1 99.5 us: local(): pl.pallas_call(functools.partial(scale_kernel, n_dp, n_code), out_shape=(...]
    unnamed x0 -> x10, local copies, waits for them, and re-layouts: none -> 3.14 us
where the time goes in v4:
time: 146 us; the launch traced here: 144 us
  Pallas kernels  140 us (96%)
  local copies, waits for them, and re-layouts  3.14 us (2%)
    pallas_call x1, Pallas kernels, local(): pl.pallas_call(functools.partial(scale_kernel, n_dp, n_code), out_shape=(...  99.5 us
    pallas_call x1, Pallas kernels, local(): pl.pallas_call(functools.partial(halo_kernel, n_dp), out_shape=shape((3,...  12.6 us
    pallas_call x1, Pallas kernels, local(): pl.pallas_call(functools.partial(exchange_kernel, n_dp), out_shape=(shape...  11.5 us
    pallas_call x1, Pallas kernels, local(): pl.pallas_call(functools.partial(score_kernel, n_dp), grid=(blocks,), out...  7.13 us
    pallas_call x1, Pallas kernels, local(): pl.pallas_call(functools.partial(sum_kernel, n_dp), grid=(blocks,), out_s...  6.99 us
    unnamed x10, local copies, waits for them, and re-layouts  3.14 us

profile of v4, /device:TPU:1, one launch (start us, length us, event | category | flops | bytes accessed | tf_op | source)
XLA Modules:
  0.0 143.6 jit_solution(344818211273725966)
XLA Ops:
  0.6 0.0 copy-start.1
  0.6 1.0 copy-done.1
  1.6 12.6 %halo.1.win_ref = bf16[3,256,768]{2,1,0:T(8,128)(2,1)S(1)} custom-call(bf16[256,768]{1,0:T(8,128)(2,1)S(1)} %copy-done.1), custom_call_target="tpu_custom_call" | custom-call | tf_op jit(solution)/shard_map/halo/pallas_call | solution.py:437
  14.2 0.0 copy-start.2
  14.2 0.7 copy-done.2
  14.9 7.1 %score.1 = (bf16[8,256,512]{2,1,0:T(8,128)(2,1)S(1)}, f32[3,256,128]{2,1,0:T(8,128)S(1)}) custom-call(s32[8,32]{1,0:T(8,128)S(1)} %copy-done.2, bf16[3,256,768]{2,1,0:T(8,128)(2,1)S(1)} %halo.1.win_ref, bf16[4096,768]{1,0:T(8,128)(2,1)} %feat_ref.3), custom_call_target="tpu_custom_call" | custom-call | tf_op jit(solution)/shard_map/score/pallas_call | solution.py:448
  22.1 0.0 copy-start.3
  22.1 99.5 %scale.1 = (bf16[8,256,512]{2,1,0:T(8,128)(2,1)S(1)}, f32[3,2,128]{2,1,0:T(2,128)S(1)}) custom-call(s32[8,32]{1,0:T(8,128)S(1)} %copy-done.2, bf16[8,256,512]{2,1,0:T(8,128)(2,1)S(1)} %get-tuple-element.10.inner_ref, f32[3,256,128]{2,1,0:T(8,128)S(1)} %get-tuple-element.11.bias_ref), custom_call_target="tpu_custom_call" | custom-call | tf_op jit(solution)/shard_map/scale/pallas_call | solution.py:458
  121.6 0.0 copy-done.3
  121.6 7.0 %sums.1.num_ref = bf16[3,256,768]{2,1,0:T(8,128)(2,1)S(1)} custom-call(s32[8,32]{1,0:T(8,128)S(1)} %copy-done.3, bf16[8,256,512]{2,1,0:T(8,128)(2,1)S(1)} %get-tuple-element.12.weight_ref, bf16[4096,768]{1,0:T(8,128)(2,1)} %feat_ref.3), custom_call_target="tpu_custom_call" | custom-call | tf_op jit(solution)/shard_map/sums/pallas_call | solution.py:495
  128.6 11.5 %exchange.1 = (f32[256,768]{1,0:T(8,128)S(1)}, f32[2,128]{1,0:T(2,128)S(1)}) custom-call(bf16[3,256,768]{2,1,0:T(8,128)(2,1)S(1)} %sums.1.num_ref, f32[3,2,128]{2,1,0:T(2,128)S(1)} %get-tuple-element.13.mass_ref), custom_call_target="tpu_custom_call" | custom-call | tf_op jit(solution)/shard_map/exchange/pallas_call | solution.py:505
  140.1 0.0 copy-start
  140.1 0.9 copy-done
  141.0 0.0 copy-start.4
  141.0 0.6 copy-done.4
  141.6 2.0 %divide.1 = (bf16[256,768]{1,0:T(8,128)(2,1)}, f32[2,128]{1,0:T(2,128)}) custom-call(f32[256,768]{1,0:T(8,128)} %copy-done, f32[2,128]{1,0:T(2,128)} %copy-done.4), custom_call_target="tpu_custom_call" | custom-call | tf_op jit(solution)/shard_map/divide/pallas_call | solution.py:523
Async XLA Ops:
  0.6 1.0 copy-start.1
  14.2 0.7 copy-start.2
  22.1 99.5 %copy-start.3 = (s32[8,32]{1,0:T(8,128)S(1)}, s32[8,32]{1,0:T(8,128)}, u32[]{:S(2)}) copy-start(s32[8,32]{1,0:T(8,128)} %lists_ref.5) | copy-start | bytes 3076
  140.1 0.9 copy-start
  141.0 0.6 copy-start.4

commit v5 on v3

--- a/solution.py
+++ b/solution.py
@@ -94,6 +94,7 @@
         other = lax.rem(share + step, shares)
         at = lax.div(other, NEAR) * Z + quarter * NEAR + lax.rem(other, NEAR)
         mates.append((other, at))
+    owners = [(b // NEAR) * Z + quarter * NEAR + b % NEAR for b in range(shares)]
     far_mates = []
     for step in range(1, quarters):
         far_mates.append(y_hi * Z + lax.rem(quarter + step, quarters) * NEAR + near)
@@ -155,9 +156,7 @@
     )
 
     def to_lanes(column):
-        square = column.reshape(3 * halves, LANES, LANES)
-        flat = jnp.sum(jnp.where(eye[None], square, 0.0), axis=1)
-        return flat.reshape(3, halves, LANES)
+        return jnp.sum(jnp.where(eye[None], column, 0.0), axis=1)
 
     def to_column(row):
         square = jnp.where(eye, jnp.broadcast_to(row, (LANES, LANES)), 0.0)
@@ -195,16 +194,20 @@
         return m + jnp.log2(jnp.sum(jnp.exp2(parts - m[None]), axis=0))
 
     def row_update(r):
-        def two_blocks(step, carry):
-            row_block(r, 2 * step)
-            row_block(r, 2 * step + 1)
-            return carry
-
-        lax.fori_loop(0, blocks // 2, two_blocks, 0)
-        for b, to in mates:
-            remote(
-                lse_src.at[r, b], lse_in.at[r, share], lse_send.at[r], lse_recv.at[r], dp, to
-            ).start()
+        for b in range(blocks):
+            row_block(r, b)
+
+            @pl.when(share != b)
+            def _():
+                remote(
+                    lse_src.at[r, b],
+                    lse_in.at[r, share],
+                    lse_send.at[r],
+                    lse_recv.at[r],
+                    dp,
+                    owners[b],
+                ).start()
+
         lse_in[r, share] = lse_src[r, share]
         others = pl.ds(0, shares - 1)
         first = remote(
@@ -227,85 +230,119 @@
         row_src[r] = value
         for _, to in mates:
             remote(
-                row_src.at[r], row_in.at[r, share], row_send.at[r], row_recv.at[r], dp, to
+                row_src.at[r], row_in.at[r, share], row_send.at[r], row_recv.at[r, share], dp, to
             ).start()
         row_in[r, share] = value
-        first.wait_send()
-        second.wait_send()
-        third = remote(
-            row_in.at[r, others], row_in.at[r, others], row_send.at[r], row_recv.at[r], dp, code
-        )
-        third.wait_recv()
-        for b in range(blocks):
+
+    def row_arrives(r, some):
+        for b in some:
+
+            @pl.when(share != b)
+            def _():
+                remote(
+                    row_src.at[r], row_in.at[r, b], row_send.at[r], row_recv.at[r, b], dp, code
+                ).wait_recv()
+
             for t in range(block_tiles):
                 row_b[b * block_tiles + t] = jnp.broadcast_to(
                     row_in[r, b, t : t + 1, :], (SUB, LANES)
                 )
-        third.wait_send()
+
+    def row_sent(r):
+        others, some = pl.ds(0, shares - 1), pl.ds(0, quarters - 1)
+        remote(
+            lse_src.at[r, others], lse_in.at[r, others], lse_send.at[r], lse_recv.at[r], dp, code
+        ).wait_send()
+        remote(
+            mid_in.at[r, some], mid_in.at[r, some], mid_send.at[r], mid_recv.at[r], dp, code
+        ).wait_send()
+        remote(
+            row_in.at[r, others], row_in.at[r, others], row_send.at[r], row_recv.at[r, 0], dp, code
+        ).wait_send()
 
     def col_update(r, target):
-        def one_tile(j):
+        def one_tile(j, some):
             span = pl.ds(pl.multiple_of(j * SUB, SUB), SUB)
-            x = cells[:, span, :] + row_b[...]
-            x = x.reshape(blocks, block_tiles, SUB, LANES)
-            at = [jnp.full((SUB, LANES), places[b], jnp.int32) for b in range(blocks)]
-            tops = [jnp.max(x[b], axis=0) for b in range(blocks)]
-            peaks = []
+            tiles_of = pl.ds(some[0] * block_tiles, len(some) * block_tiles)
+            x = cells[tiles_of, span, :] + row_b[tiles_of]
+            x = x.reshape(len(some), block_tiles, SUB, LANES)
+            at = [jnp.full((SUB, LANES), places[b], jnp.int32) for b in some]
+            tops = [jnp.max(x[i], axis=0) for i in range(len(some))]
+            peaks, olds = [], []
             for w in range(3):
-                held = [jnp.where(at[b] == w, tops[b], LOWEST) for b in range(blocks)]
+                held = [jnp.where(at[i] == w, tops[i], LOWEST) for i in range(len(some))]
+                if some[0] > 0:
+                    olds.append(peak[w, span, :])
+                    held.append(olds[w])
                 peaks.append(functools.reduce(jnp.maximum, held))
             sums = []
-            for b in range(blocks):
-                top = jnp.where(at[b] == 0, peaks[0], jnp.where(at[b] == 1, peaks[1], peaks[2]))
-                sums.append(jnp.sum(jnp.exp2(x[b] - top[None]), axis=0))
+            for i in range(len(some)):
+                top = jnp.where(at[i] == 0, peaks[0], jnp.where(at[i] == 1, peaks[1], peaks[2]))
+                sums.append(jnp.sum(jnp.exp2(x[i] - top[None]), axis=0))
             for w in range(3):
-                held = [jnp.where(at[b] == w, sums[b], 0.0) for b in range(blocks)]
+                held = [jnp.where(at[i] == w, sums[i], 0.0) for i in range(len(some))]
+                if some[0] > 0:
+                    held.append(total[w, span, :] * jnp.exp2(olds[w] - peaks[w]))
                 peak[w, span, :] = peaks[w]
                 total[w, span, :] = functools.reduce(jnp.add, held)
 
-        def two_tiles(j, carry):
-            one_tile(2 * j)
-            one_tile(2 * j + 1)
-            return carry
-
-        lax.fori_loop(0, size // SUB // 2, two_tiles, 0)
-        m = jnp.max(peak[...], axis=2, keepdims=True)
-        s = jnp.sum(total[...] * jnp.exp2(peak[...] - m), axis=2, keepdims=True)
-        mine = to_lanes(jnp.broadcast_to(m, peak.shape)) + jnp.log2(
-            to_lanes(jnp.broadcast_to(s, total.shape))
-        )
-        col_src[r] = mine
-        copies = [
-            remote(
-                col_src.at[r, pl.ds(start, count)],
-                there.at[r],
-                col_send.at[r, slot],
-                col_recv.at[r, slot],
-                dp_near[step],
-                code,
+        def tile_loop(first, last, some):
+            def two_tiles(j, carry):
+                one_tile(2 * j, some)
+                one_tile(2 * j + 1, some)
+                return carry
+
+            lax.fori_loop(first // 2, last // 2, two_tiles, 0)
+
+        half_tiles = LANES // SUB
+        early, late = range(blocks // 2), range(blocks // 2, blocks)
+        row_arrives(r, early)
+        tile_loop(0, size // SUB, early)
+        row_arrives(r, late)
+        mines, copies = [], []
+        for h in range(halves):
+            tile_loop(h * half_tiles, (h + 1) * half_tiles, late)
+            span = slice(h * LANES, (h + 1) * LANES)
+            tops, sums = peak[:, span, :], total[:, span, :]
+            m = jnp.max(tops, axis=2, keepdims=True)
+            s = jnp.sum(sums * jnp.exp2(tops - m), axis=2, keepdims=True)
+            mine = to_lanes(jnp.broadcast_to(m, tops.shape)) + jnp.log2(
+                to_lanes(jnp.broadcast_to(s, sums.shape))
             )
+            mines.append(mine)
+            for w in range(3):
+                col_src[r, h, w] = mine[w : w + 1]
             for slot, (step, start, count, there) in enumerate(
                 ((-2, 0, 1, col_r2), (2, 2, 1, col_l2), (-1, 0, 2, col_r1), (1, 1, 2, col_l1))
+            ):
+                copies.append(
+                    remote(
+                        col_src.at[r, h, pl.ds(start, count)],
+                        there.at[r, h],
+                        col_send.at[r, h, slot],
+                        col_recv.at[r, h, slot],
+                        dp_near[step],
+                        code,
+                    )
+                )
+                copies[-1].start()
+        for h in range(halves):
+            for copy in copies[4 * h : 4 * h + 4]:
+                copy.wait_recv()
+            mine, l1, r1 = mines[h], col_l1[r, h], col_r1[r, h]
+            sets = (
+                (col_l2[r, h, 0], l1[0], mine[0:1]),
+                (l1[1], mine[1:2], r1[0]),
+                (mine[2:3], r1[1], col_r2[r, h, 0]),
             )
-        ]
-        for copy in copies:
-            copy.start()
-        for copy in copies:
-            copy.wait_recv()
-        l1, r1 = col_l1[r], col_r1[r]
-        sets = (
-            (col_l2[r, 0], l1[0], mine[0]),
-            (l1[1], mine[1], r1[0]),
-            (mine[2], r1[1], col_r2[r, 0]),
-        )
-        for w, terms in enumerate(sets):
-            m = functools.reduce(jnp.maximum, terms)
-            s = functools.reduce(jnp.add, [jnp.exp2(term - m) for term in terms])
-            value = target - (m + jnp.log2(s))
-            for h in range(halves):
-                col_b[w, h * LANES : (h + 1) * LANES, :] = to_column(value[h : h + 1])
+            for w, terms in enumerate(sets):
+                m = functools.reduce(jnp.maximum, terms)
+                s = functools.reduce(jnp.add, [jnp.exp2(term - m) for term in terms])
+                value = target - (m + jnp.log2(s))
+                col_b[w, h * LANES : (h + 1) * LANES, :] = to_column(value)
         for copy in copies:
             copy.wait_send()
+        row_sent(r)
 
     target = math.log2((rows * n_dp) / (size * n_dp * n_code))
 
@@ -316,6 +353,8 @@
 
     lax.fori_loop(0, ROUNDS, sweep, 0)
     row_update(ROUNDS)
+    row_arrives(ROUNDS, range(blocks))
+    row_sent(ROUNDS)
 
     pack = 2 * SUB
 
@@ -342,8 +381,10 @@
     lax.fori_loop(0, size // pack, weigh, 0)
 
     mass = jnp.sum(total[...], axis=2, keepdims=True)
-    mass = to_lanes(jnp.broadcast_to(mass, total.shape))
-    mass_src[...] = mass.astype(jnp.bfloat16).astype(jnp.float32)
+    mass = jnp.broadcast_to(mass, total.shape)
+    for h in range(halves):
+        part = to_lanes(mass[:, h * LANES : (h + 1) * LANES, :])
+        mass_src[:, h, :] = part.astype(jnp.bfloat16).astype(jnp.float32)
     mass_copies = [
         remote(
             mass_src.at[pl.ds(2 * s, 1)],
@@ -479,11 +520,11 @@
                 pltpu.VMEM((updates, Z // NEAR, block_tiles, LANES), f32),
                 pltpu.VMEM((updates, block_tiles, LANES), f32),
                 pltpu.VMEM((updates, blocks, block_tiles, LANES), f32),
-                pltpu.VMEM((ROUNDS, 3, halves, LANES), f32),
-                pltpu.VMEM((ROUNDS, 1, halves, LANES), f32),
-                pltpu.VMEM((ROUNDS, 2, halves, LANES), f32),
-                pltpu.VMEM((ROUNDS, 2, halves, LANES), f32),
-                pltpu.VMEM((ROUNDS, 1, halves, LANES), f32),
+                pltpu.VMEM((ROUNDS, halves, 3, 1, LANES), f32),
+                pltpu.VMEM((ROUNDS, halves, 1, 1, LANES), f32),
+                pltpu.VMEM((ROUNDS, halves, 2, 1, LANES), f32),
+                pltpu.VMEM((ROUNDS, halves, 2, 1, LANES), f32),
+                pltpu.VMEM((ROUNDS, halves, 1, 1, LANES), f32),
                 pltpu.VMEM((3, halves, LANES), f32),
                 pltpu.VMEM((2, 1, halves, LANES), f32),
                 pltpu.VMEM((2, PIECES, size, piece), bf16),
@@ -498,9 +539,9 @@
                 dma((updates,)),
                 dma((updates,)),
                 dma((updates,)),
-                dma((updates,)),
-                dma((ROUNDS, 4)),
-                dma((ROUNDS, 4)),
+                dma((updates, blocks)),
+                dma((ROUNDS, halves, 4)),
+                dma((ROUNDS, halves, 4)),
                 dma((2,)),
                 dma((2,)),
                 dma((2, PIECES)),

time: 129 us -> 128 us (level)
  no operation moved by 1% of the time
where the time goes in v5:
time: 128 us
  Pallas kernels  127 us (99%)
    pallas_call x1, Pallas kernels, local(): pl.pallas_call(functools.partial(kernel, n_dp, n_code), out_shape=(jax.Sh...  125 us

profile of v5, /device:TPU:1, one launch (start us, length us, event | category | flops | bytes accessed | tf_op | source)
XLA Modules:
  0.0 127.7 jit_solution(4800893443346834364)
XLA Ops:
  0.6 125.0 %balanced_kmeans.1 = (f32[3,256,256]{2,1,0:T(8,128)}, f32[2,128]{1,0:T(2,128)}) custom-call(s32[8,32]{1,0:T(8,128)} %lists_ref.1, bf16[4096,768]{1,0:T(8,128)(2,1)} %feat_hbm.1, bf16[256,768]{1,0:T(8,128)(2,1)} %cent_hbm.1), custom_call_target="tpu_custom_call" | custom-call | flops 6442450944 | bytes 7077888 | tf_op jit(solution)/shard_map/balanced_kmeans/pallas_call | solution.py:492
  125.7 2.0 %divide.1 = (bf16[256,768]{1,0:T(8,128)(2,1)}, f32[2,128]{1,0:T(2,128)}) custom-call(f32[3,256,256]{2,1,0:T(8,128)} %get-tuple-element.6.whole_ref, f32[2,128]{1,0:T(2,128)} %get-tuple-element.7.mass_in_ref), custom_call_target="tpu_custom_call" | custom-call | flops 196608 | bytes 1179648 | tf_op jit(solution)/shard_map/divide/pallas_call | solution.py:560

commit v6 on v5

--- a/solution.py
+++ b/solution.py
@@ -16,7 +16,7 @@
 SUB = 8
 PIECES = 3
 Z = 16
-NEAR = 4
+NEAR = 2
 MESH = pl.DeviceIdType.MESH
 
 
@@ -89,6 +89,7 @@
     quarter, near = lax.div(z, NEAR), lax.rem(z, NEAR)
     quarters, shares = Z // NEAR, NEAR * (n_code // Z)
     share = y_hi * NEAR + near
+    held = blocks // shares
     mates = []
     for step in range(1, shares):
         other = lax.rem(share + step, shares)
@@ -96,7 +97,7 @@
         mates.append((other, at))
     owners = [(b // NEAR) * Z + quarter * NEAR + b % NEAR for b in range(shares)]
     far_mates = []
-    for step in range(1, quarters):
+    for step in sorted(range(1, quarters), key=lambda step: abs(2 * step - quarters)):
         far_mates.append(y_hi * Z + lax.rem(quarter + step, quarters) * NEAR + near)
 
     def feat_copy(b):
@@ -179,7 +180,8 @@
     norms(0)
     norms(2)
 
-    def row_block(r, b):
+    def row_block(r, owner, i):
+        b = owner * held + i
         bias = col_b[places[b]]
         for t in range(block_tiles):
             x = (cells[b * block_tiles + t] + bias).reshape(size // SUB, SUB, LANES)
@@ -187,25 +189,26 @@
             s8 = jnp.sum(jnp.exp2(x - m8[None]), axis=0)
             m = jnp.max(m8, axis=0, keepdims=True)
             s = jnp.sum(s8 * jnp.exp2(m8 - m), axis=0, keepdims=True)
-            lse_src[r, b, t : t + 1, :] = m + jnp.log2(s)
+            lse_src[r, owner, i, t : t + 1, :] = m + jnp.log2(s)
 
     def join(parts):
         m = jnp.max(parts, axis=0)
         return m + jnp.log2(jnp.sum(jnp.exp2(parts - m[None]), axis=0))
 
     def row_update(r):
-        for b in range(blocks):
-            row_block(r, b)
-
-            @pl.when(share != b)
+        for owner in range(shares):
+            for b in range(owner * held, (owner + 1) * held):
+                row_block(r, owner, b - owner * held)
+
+            @pl.when(share != owner)
             def _():
                 remote(
-                    lse_src.at[r, b],
+                    lse_src.at[r, owner],
                     lse_in.at[r, share],
                     lse_send.at[r],
                     lse_recv.at[r],
                     dp,
-                    owners[b],
+                    owners[owner],
                 ).start()
 
         lse_in[r, share] = lse_src[r, share]
@@ -235,18 +238,24 @@
         row_in[r, share] = value
 
     def row_arrives(r, some):
-        for b in some:
-
-            @pl.when(share != b)
+        for owner in range(some[0] // held, some[-1] // held + 1):
+
+            @pl.when(share != owner)
             def _():
                 remote(
-                    row_src.at[r], row_in.at[r, b], row_send.at[r], row_recv.at[r, b], dp, code
+                    row_src.at[r],
+                    row_in.at[r, owner],
+                    row_send.at[r],
+                    row_recv.at[r, owner],
+                    dp,
+                    code,
                 ).wait_recv()
 
-            for t in range(block_tiles):
-                row_b[b * block_tiles + t] = jnp.broadcast_to(
-                    row_in[r, b, t : t + 1, :], (SUB, LANES)
-                )
+            for i in range(held):
+                for t in range(block_tiles):
+                    row_b[(owner * held + i) * block_tiles + t] = jnp.broadcast_to(
+                        row_in[r, owner, i, t : t + 1, :], (SUB, LANES)
+                    )
 
     def row_sent(r):
         others, some = pl.ds(0, shares - 1), pl.ds(0, quarters - 1)
@@ -270,21 +279,21 @@
             tops = [jnp.max(x[i], axis=0) for i in range(len(some))]
             peaks, olds = [], []
             for w in range(3):
-                held = [jnp.where(at[i] == w, tops[i], LOWEST) for i in range(len(some))]
+                kept = [jnp.where(at[i] == w, tops[i], LOWEST) for i in range(len(some))]
                 if some[0] > 0:
                     olds.append(peak[w, span, :])
-                    held.append(olds[w])
-                peaks.append(functools.reduce(jnp.maximum, held))
+                    kept.append(olds[w])
+                peaks.append(functools.reduce(jnp.maximum, kept))
             sums = []
             for i in range(len(some)):
                 top = jnp.where(at[i] == 0, peaks[0], jnp.where(at[i] == 1, peaks[1], peaks[2]))
                 sums.append(jnp.sum(jnp.exp2(x[i] - top[None]), axis=0))
             for w in range(3):
-                held = [jnp.where(at[i] == w, sums[i], 0.0) for i in range(len(some))]
+                kept = [jnp.where(at[i] == w, sums[i], 0.0) for i in range(len(some))]
                 if some[0] > 0:
-                    held.append(total[w, span, :] * jnp.exp2(olds[w] - peaks[w]))
+                    kept.append(total[w, span, :] * jnp.exp2(olds[w] - peaks[w]))
                 peak[w, span, :] = peaks[w]
-                total[w, span, :] = functools.reduce(jnp.add, held)
+                total[w, span, :] = functools.reduce(jnp.add, kept)
 
         def tile_loop(first, last, some):
             def two_tiles(j, carry):
@@ -426,8 +435,8 @@
                 )
                 products.append((jnp.full(product.shape, places[b], jnp.int32), product))
             for w in range(3):
-                held = [jnp.where(at == w, product, 0.0) for at, product in products]
-                num_sum[n, w] = num_sum[n, w] + (held[0] + held[1])
+                kept = [jnp.where(at == w, product, 0.0) for at, product in products]
+                num_sum[n, w] = num_sum[n, w] + (kept[0] + kept[1])
             return carry
 
         lax.fori_loop(0, blocks // 2, two_blocks, 0)
@@ -484,6 +493,8 @@
         tiles = rows // LANES
         blocks = block_lists.shape[0]
         block_tiles = tiles // blocks
+        shares = NEAR * (n_code // Z)
+        mine = (blocks // shares, block_tiles, LANES)
         halves = size // LANES
         piece = width // PIECES
         updates = ROUNDS + 1
@@ -514,12 +525,12 @@
                 pltpu.VMEM((3, size, LANES), f32),
                 pltpu.VMEM((blocks, size, rows // blocks), bf16),
                 pltpu.SMEM((blocks,), jnp.int32),
-                pltpu.VMEM((updates, blocks, block_tiles, LANES), f32),
-                pltpu.VMEM((updates, blocks, block_tiles, LANES), f32),
-                pltpu.VMEM((updates, block_tiles, LANES), f32),
-                pltpu.VMEM((updates, Z // NEAR, block_tiles, LANES), f32),
-                pltpu.VMEM((updates, block_tiles, LANES), f32),
-                pltpu.VMEM((updates, blocks, block_tiles, LANES), f32),
+                pltpu.VMEM((updates, shares, *mine), f32),
+                pltpu.VMEM((updates, shares, *mine), f32),
+                pltpu.VMEM((updates, *mine), f32),
+                pltpu.VMEM((updates, Z // NEAR, *mine), f32),
+                pltpu.VMEM((updates, *mine), f32),
+                pltpu.VMEM((updates, shares, *mine), f32),
                 pltpu.VMEM((ROUNDS, halves, 3, 1, LANES), f32),
                 pltpu.VMEM((ROUNDS, halves, 1, 1, LANES), f32),
                 pltpu.VMEM((ROUNDS, halves, 2, 1, LANES), f32),
@@ -539,7 +550,7 @@
                 dma((updates,)),
                 dma((updates,)),
                 dma((updates,)),
-                dma((updates, blocks)),
+                dma((updates, shares)),
                 dma((ROUNDS, halves, 4)),
                 dma((ROUNDS, halves, 4)),
                 dma((2,)),

time: 128 us -> 120 us (0.938)
  Pallas kernels: 127 us -> 120 us
    pallas_call x1, Pallas kernels: 125 us -> 118 us  [local(): pl.pallas_call(functools.partial(kernel, n_dp, n_code), out_shape=(jax.Sh...]
where the time goes in v6:
time: 120 us
  Pallas kernels  120 us (100%)
    pallas_call x1, Pallas kernels, local(): pl.pallas_call(functools.partial(kernel, n_dp, n_code), out_shape=(jax.Sh...  118 us

profile of v6, /device:TPU:1, one launch (start us, length us, event | category | flops | bytes accessed | tf_op | source)
XLA Modules:
  0.0 120.2 jit_solution(13548327659892585843)
XLA Ops:
  0.6 117.5 %balanced_kmeans.1 = (f32[3,256,256]{2,1,0:T(8,128)}, f32[2,128]{1,0:T(2,128)}) custom-call(s32[8,32]{1,0:T(8,128)} %lists_ref.1, bf16[4096,768]{1,0:T(8,128)(2,1)} %feat_hbm.1, bf16[256,768]{1,0:T(8,128)(2,1)} %cent_hbm.1), custom_call_target="tpu_custom_call" | custom-call | flops 6442450944 | bytes 7077888 | tf_op jit(solution)/shard_map/balanced_kmeans/pallas_call | solution.py:503
  118.1 2.0 %divide.1 = (bf16[256,768]{1,0:T(8,128)(2,1)}, f32[2,128]{1,0:T(2,128)}) custom-call(f32[3,256,256]{2,1,0:T(8,128)} %get-tuple-element.6.whole_ref, f32[2,128]{1,0:T(2,128)} %get-tuple-element.7.mass_in_ref), custom_call_target="tpu_custom_call" | custom-call | flops 196608 | bytes 1179648 | tf_op jit(solution)/shard_map/divide/pallas_call | solution.py:571

commit v7 on v6

--- a/solution.py
+++ b/solution.py
@@ -26,10 +26,11 @@
     lists_ref,
     feat_hbm,
     cent_hbm,
-    whole_ref,
+    out_ref,
     mass_ref,
     feat,
-    win,
+    win_a,
+    win_b,
     cells,
     row_b,
     col_b,
@@ -77,8 +78,9 @@
     block_rows = rows // blocks
     block_tiles = block_rows // LANES
     tiles = rows // LANES
-    size, width = win.shape[1], win.shape[2]
-    halves = size // LANES
+    wins = (win_a, win_b)
+    halves = len(wins)
+    size, width = halves * win_a.shape[1], win_a.shape[2]
     piece = width // PIECES
     odd = lax.rem(dp, 2)
     dp_near = {step: lax.rem(dp + (n_dp + step), n_dp) for step in (-2, -1, 1, 2)}
@@ -114,8 +116,14 @@
             device_id_type=MESH,
         )
 
-    own_copy = pltpu.make_async_copy(cent_hbm, win.at[1], own_sem)
-    own_copy.start()
+    def half(h):
+        return cent_hbm.at[pl.ds(h * LANES, LANES)]
+
+    own_copies = [
+        pltpu.make_async_copy(half(h), wins[h].at[1], own_sem.at[h]) for h in range(halves)
+    ]
+    for copy in own_copies:
+        copy.start()
     for b in range(blocks):
         feat_copy(b).start()
 
@@ -131,26 +139,31 @@
     ups = (odd, 1 - odd)
     sides = [dp_near[-1] + up * (dp_near[1] - dp_near[-1]) for up in ups]
 
-    def halo(s):
+    def halo(s, h):
         land = 1 - ups[s]
         return remote(
-            cent_hbm, win.at[2 * land], halo_send.at[s], halo_recv.at[land], sides[s], code
-        )
-
-    halo(0).start()
-    halo(1).start()
-
-    def norms(w):
-        wide = win[w].astype(jnp.float32)
+            half(h),
+            wins[h].at[2 * land],
+            halo_send.at[s, h],
+            halo_recv.at[land, h],
+            sides[s],
+            code,
+        )
+
+    halos = [halo(s, h) for h in range(halves) for s in range(2)]
+    for copy in halos:
+        copy.start()
+
+    def norms(w, h):
+        wide = wins[h][w].astype(jnp.float32)
         norm = jnp.sum(wide * wide, axis=1, keepdims=True)
-        col_b[w] = jnp.broadcast_to(norm * (-LOG2E / SOFTMAX_TEMP), (size, LANES))
-
-    own_copy.wait()
-    norms(1)
-    for s in range(2):
-        halo(s).wait_send()
-    for s in range(2):
-        remote(cent_hbm, win.at[2 * s], halo_send.at[s], halo_recv.at[s], dp, code).wait_recv()
+        col_b[w, h * LANES : (h + 1) * LANES, :] = jnp.broadcast_to(
+            norm * (-LOG2E / SOFTMAX_TEMP), (LANES, LANES)
+        )
+
+    for h in range(halves):
+        own_copies[h].wait()
+        norms(1, h)
 
     eye = lax.broadcasted_iota(jnp.int32, (LANES, LANES), 0) == lax.broadcasted_iota(
         jnp.int32, (LANES, LANES), 1
@@ -163,22 +176,33 @@
         square = jnp.where(eye, jnp.broadcast_to(row, (LANES, LANES)), 0.0)
         return jnp.broadcast_to(jnp.sum(square, axis=1, keepdims=True), (LANES, LANES))
 
-    def score(b, carry):
-        feat_copy(b).wait()
-        inner = lax.dot_general(
-            win[places[b]],
-            feat[pl.ds(pl.multiple_of(b * block_rows, block_rows), block_rows), :],
-            (((1,), (1,)), ((), ())),
-            preferred_element_type=jnp.float32,
-        )
-        scaled = inner.astype(jnp.bfloat16).astype(jnp.float32) * (2.0 * LOG2E / SOFTMAX_TEMP)
-        for t in range(block_tiles):
-            cells[b * block_tiles + t] = scaled[:, t * LANES : (t + 1) * LANES]
-        return carry
-
-    lax.fori_loop(0, blocks, score, 0)
-    norms(0)
-    norms(2)
+    for h in range(halves):
+        for s in range(2):
+            remote(
+                half(h), wins[h].at[2 * s], halo_send.at[s, h], halo_recv.at[s, h], dp, code
+            ).wait_recv()
+
+        def score(b, carry):
+            if h == 0:
+                feat_copy(b).wait()
+            inner = lax.dot_general(
+                wins[h][places[b]],
+                feat[pl.ds(pl.multiple_of(b * block_rows, block_rows), block_rows), :],
+                (((1,), (1,)), ((), ())),
+                preferred_element_type=jnp.float32,
+            )
+            scaled = inner.astype(jnp.bfloat16).astype(jnp.float32) * (2.0 * LOG2E / SOFTMAX_TEMP)
+            for t in range(block_tiles):
+                cells[b * block_tiles + t, h * LANES : (h + 1) * LANES, :] = scaled[
+                    :, t * LANES : (t + 1) * LANES
+                ]
+            return carry
+
+        lax.fori_loop(0, blocks, score, 0)
+        norms(0, h)
+        norms(2, h)
+    for copy in halos:
+        copy.wait_send()
 
     def row_block(r, owner, i):
         b = owner * held + i
@@ -362,32 +386,36 @@
 
     lax.fori_loop(0, ROUNDS, sweep, 0)
     row_update(ROUNDS)
-    row_arrives(ROUNDS, range(blocks))
+    pack = 2 * SUB
+
+    def weigh(some):
+        def body(j, carry):
+            span = pl.ds(pl.multiple_of(j * pack, pack), pack)
+            sums = [jnp.zeros((2, SUB, LANES), jnp.float32) for w in range(3)]
+            for b in some:
+                g = col_b[places[b], span, :].reshape(2, SUB, LANES)
+                here = jnp.zeros((2, SUB, LANES), jnp.float32)
+                for t in range(block_tiles):
+                    d = b * block_tiles + t
+                    x = cells[d, span, :].reshape(2, SUB, LANES) + row_b[d][None] + g
+                    value = jnp.exp2(x)
+                    here = here + value
+                    low = value.reshape(pack, LANES).astype(jnp.bfloat16)
+                    weight[b, span, t * LANES : (t + 1) * LANES] = low
+                at = jnp.full((2, SUB, LANES), places[b], jnp.int32)
+                for w in range(3):
+                    sums[w] = sums[w] + jnp.where(at == w, here, 0.0)
+            for w in range(3):
+                part = sums[w].reshape(pack, LANES)
+                total[w, span, :] = part if some[0] == 0 else total[w, span, :] + part
+            return carry
+
+        lax.fori_loop(0, size // pack, body, 0)
+
+    for some in (range(blocks // 2), range(blocks // 2, blocks)):
+        row_arrives(ROUNDS, some)
+        weigh(some)
     row_sent(ROUNDS)
-
-    pack = 2 * SUB
-
-    def weigh(j, carry):
-        span = pl.ds(pl.multiple_of(j * pack, pack), pack)
-        sums = [jnp.zeros((2, SUB, LANES), jnp.float32) for w in range(3)]
-        for b in range(blocks):
-            g = col_b[places[b], span, :].reshape(2, SUB, LANES)
-            here = jnp.zeros((2, SUB, LANES), jnp.float32)
-            for t in range(block_tiles):
-                d = b * block_tiles + t
-                x = cells[d, span, :].reshape(2, SUB, LANES) + row_b[d][None] + g
-                value = jnp.exp2(x)
-                here = here + value
-                low = value.reshape(pack, LANES).astype(jnp.bfloat16)
-                weight[b, span, t * LANES : (t + 1) * LANES] = low
-            at = jnp.full((2, SUB, LANES), places[b], jnp.int32)
-            for w in range(3):
-                sums[w] = sums[w] + jnp.where(at == w, here, 0.0)
-        for w in range(3):
-            total[w, span, :] = sums[w].reshape(pack, LANES)
-        return carry
-
-    lax.fori_loop(0, size // pack, weigh, 0)
 
     mass = jnp.sum(total[...], axis=2, keepdims=True)
     mass = jnp.broadcast_to(mass, total.shape)
@@ -453,7 +481,10 @@
         ).wait_recv()
     for copy in mass_copies:
         copy.wait_send()
-    mass_ref[...] = mass_in[0, 0] + mass_src[1] + mass_in[1, 0]
+    mass_all = mass_in[0, 0] + mass_src[1] + mass_in[1, 0]
+    mass_ref[...] = mass_all
+    for h in range(halves):
+        peak[0, h * LANES : (h + 1) * LANES, :] = to_column(mass_all[h : h + 1])
 
     def finish(n, carry):
         for s in range(2):
@@ -461,27 +492,23 @@
                 num_src.at[s, n], num_in.at[s, n], num_send.at[s, n], num_recv.at[s, n], dp, code
             ).wait()
         own = num_sum[n, 1].astype(jnp.bfloat16).astype(jnp.float32)
-        whole_ref[n] = (
-            num_in[0, n].astype(jnp.float32) + own + num_in[1, n].astype(jnp.float32)
-        )
+        whole = num_in[0, n].astype(jnp.float32) + own + num_in[1, n].astype(jnp.float32)
+        divisor = jnp.concatenate([peak[0]] * (piece // LANES), axis=1)
+        out_ref[:, columns(n)] = (whole / divisor).astype(jnp.bfloat16)
         return carry
 
     lax.fori_loop(0, PIECES, finish, 0)
 
 
-def divide(whole_ref, mass_in_ref, out_ref, mass_ref):
-    size, piece = whole_ref.shape[1], whole_ref.shape[2]
-    eye = lax.broadcasted_iota(jnp.int32, (LANES, LANES), 0) == lax.broadcasted_iota(
-        jnp.int32, (LANES, LANES), 1
-    )
-    mass_ref[...] = mass_in_ref[...]
-    for h in range(size // LANES):
-        row = jnp.broadcast_to(mass_in_ref[h : h + 1, :], (LANES, LANES))
-        column = jnp.sum(jnp.where(eye, row, 0.0), axis=1, keepdims=True)
-        span = slice(h * LANES, (h + 1) * LANES)
-        for n in range(PIECES):
-            value = whole_ref[n, span, :] / column
-            out_ref[span, n * piece : (n + 1) * piece] = value.astype(out_ref.dtype)
+def pass_on(new_ref, mass_in_ref, out_ref, mass_ref, sems):
+    copies = [
+        pltpu.make_async_copy(new_ref, out_ref, sems.at[0]),
+        pltpu.make_async_copy(mass_in_ref, mass_ref, sems.at[1]),
+    ]
+    for copy in copies:
+        copy.start()
+    for copy in copies:
+        copy.wait()
 
 
 def solution(mesh):
@@ -500,10 +527,10 @@
         updates = ROUNDS + 1
         f32, bf16 = jnp.float32, jnp.bfloat16
         dma = pltpu.SemaphoreType.DMA
-        whole, mass = pl.pallas_call(
+        new_centroids, mass = pl.pallas_call(
             functools.partial(kernel, n_dp, n_code),
             out_shape=(
-                jax.ShapeDtypeStruct((PIECES, size, piece), f32),
+                jax.ShapeDtypeStruct((size, width), bf16),
                 jax.ShapeDtypeStruct((halves, LANES), f32),
             ),
             in_specs=[
@@ -517,7 +544,8 @@
             ),
             scratch_shapes=[
                 pltpu.VMEM((rows, width), bf16),
-                pltpu.VMEM((3, size, width), bf16),
+                pltpu.VMEM((3, size // halves, width), bf16),
+                pltpu.VMEM((3, size // halves, width), bf16),
                 pltpu.VMEM((tiles, size, LANES), f32),
                 pltpu.VMEM((tiles, SUB, LANES), f32),
                 pltpu.VMEM((3, size, LANES), f32),
@@ -542,9 +570,9 @@
                 pltpu.VMEM((2, PIECES, size, piece), bf16),
                 pltpu.VMEM((PIECES, 3, size, piece), f32),
                 dma((blocks,)),
-                dma,
-                dma((2,)),
-                dma((2,)),
+                dma((halves,)),
+                dma((2, halves)),
+                dma((2, halves)),
                 dma((updates,)),
                 dma((updates,)),
                 dma((updates,)),
@@ -569,16 +597,19 @@
             name="balanced_kmeans",
         )(block_lists, features, centroids)
         new_centroids, mass = pl.pallas_call(
-            divide,
+            pass_on,
             out_shape=(
                 jax.ShapeDtypeStruct((size, width), bf16),
                 jax.ShapeDtypeStruct((halves, LANES), f32),
             ),
+            in_specs=[pl.BlockSpec(memory_space=pl.ANY)] * 2,
+            out_specs=(pl.BlockSpec(memory_space=pl.ANY),) * 2,
+            scratch_shapes=[dma((2,))],
             cost_estimate=pl.CostEstimate(
-                flops=size * width, bytes_accessed=6 * size * width, transcendentals=0
+                flops=0, bytes_accessed=4 * size * width, transcendentals=0
             ),
-            name="divide",
-        )(whole, mass)
+            name="pass_on",
+        )(new_centroids, mass)
         return new_centroids, mass.reshape(size)
 
     return jax.shard_map(

time: 120 us -> 132 us (1.10)
  Pallas kernels: 120 us -> 131 us
    pallas_call x1, Pallas kernels: 2.02 us -> 13.1 us  [local(): pl.pallas_call(pass_on, out_shape=(jax.ShapeDtypeStruct((size, width), bf...]
where the time goes in v7:
time: 132 us
  Pallas kernels  131 us (99%)
    pallas_call x1, Pallas kernels, local(): pl.pallas_call(functools.partial(kernel, n_dp, n_code), out_shape=(jax.Sh...  118 us
    pallas_call x1, Pallas kernels, local(): pl.pallas_call(pass_on, out_shape=(jax.ShapeDtypeStruct((size, width), bf...  13.1 us

profile of v7, /device:TPU:1, one launch (start us, length us, event | category | flops | bytes accessed | tf_op | source)
XLA Modules:
  0.0 131.9 jit_solution(7133512755504703636)
XLA Ops:
  0.6 118.2 %balanced_kmeans.1 = (bf16[256,768]{1,0:T(8,128)(2,1)}, f32[2,128]{1,0:T(2,128)}) custom-call(s32[8,32]{1,0:T(8,128)} %lists_ref.1, bf16[4096,768]{1,0:T(8,128)(2,1)} %feat_hbm.1, bf16[256,768]{1,0:T(8,128)(2,1)} %cent_hbm.1), custom_call_target="tpu_custom_call" | custom-call | flops 6442450944 | bytes 7077888 | tf_op jit(solution)/shard_map/balanced_kmeans/pallas_call | solution.py:530
  118.9 13.1 %pass_on.1 = (bf16[256,768]{1,0:T(8,128)(2,1)}, f32[2,128]{1,0:T(2,128)}) custom-call(bf16[256,768]{1,0:T(8,128)(2,1)} %get-tuple-element.6.new_ref, f32[2,128]{1,0:T(2,128)} %get-tuple-element.7.mass_in_ref), custom_call_target="tpu_custom_call" | custom-call | bytes 786432 | tf_op jit(solution)/shard_map/pass_on/pallas_call | solution.py:599

commit v8 on v6

--- a/solution.py
+++ b/solution.py
@@ -163,8 +163,7 @@
         square = jnp.where(eye, jnp.broadcast_to(row, (LANES, LANES)), 0.0)
         return jnp.broadcast_to(jnp.sum(square, axis=1, keepdims=True), (LANES, LANES))
 
-    def score(b, carry):
-        feat_copy(b).wait()
+    def score(b):
         inner = lax.dot_general(
             win[places[b]],
             feat[pl.ds(pl.multiple_of(b * block_rows, block_rows), block_rows), :],
@@ -174,9 +173,15 @@
         scaled = inner.astype(jnp.bfloat16).astype(jnp.float32) * (2.0 * LOG2E / SOFTMAX_TEMP)
         for t in range(block_tiles):
             cells[b * block_tiles + t] = scaled[:, t * LANES : (t + 1) * LANES]
+
+    def two_scores(step, carry):
+        feat_copy(2 * step).wait()
+        feat_copy(2 * step + 1).wait()
+        score(2 * step)
+        score(2 * step + 1)
         return carry
 
-    lax.fori_loop(0, blocks, score, 0)
+    lax.fori_loop(0, blocks // 2, two_scores, 0)
     norms(0)
     norms(2)
 
@@ -362,32 +367,36 @@
 
     lax.fori_loop(0, ROUNDS, sweep, 0)
     row_update(ROUNDS)
-    row_arrives(ROUNDS, range(blocks))
+    pack = 2 * SUB
+
+    def weigh(some):
+        def body(j, carry):
+            span = pl.ds(pl.multiple_of(j * pack, pack), pack)
+            sums = [jnp.zeros((2, SUB, LANES), jnp.float32) for w in range(3)]
+            for b in some:
+                g = col_b[places[b], span, :].reshape(2, SUB, LANES)
+                here = jnp.zeros((2, SUB, LANES), jnp.float32)
+                for t in range(block_tiles):
+                    d = b * block_tiles + t
+                    x = cells[d, span, :].reshape(2, SUB, LANES) + row_b[d][None] + g
+                    value = jnp.exp2(x)
+                    here = here + value
+                    low = value.reshape(pack, LANES).astype(jnp.bfloat16)
+                    weight[b, span, t * LANES : (t + 1) * LANES] = low
+                at = jnp.full((2, SUB, LANES), places[b], jnp.int32)
+                for w in range(3):
+                    sums[w] = sums[w] + jnp.where(at == w, here, 0.0)
+            for w in range(3):
+                part = sums[w].reshape(pack, LANES)
+                total[w, span, :] = part if some[0] == 0 else total[w, span, :] + part
+            return carry
+
+        lax.fori_loop(0, size // pack, body, 0)
+
+    for some in (range(blocks // 2), range(blocks // 2, blocks)):
+        row_arrives(ROUNDS, some)
+        weigh(some)
     row_sent(ROUNDS)
-
-    pack = 2 * SUB
-
-    def weigh(j, carry):
-        span = pl.ds(pl.multiple_of(j * pack, pack), pack)
-        sums = [jnp.zeros((2, SUB, LANES), jnp.float32) for w in range(3)]
-        for b in range(blocks):
-            g = col_b[places[b], span, :].reshape(2, SUB, LANES)
-            here = jnp.zeros((2, SUB, LANES), jnp.float32)
-            for t in range(block_tiles):
-                d = b * block_tiles + t
-                x = cells[d, span, :].reshape(2, SUB, LANES) + row_b[d][None] + g
-                value = jnp.exp2(x)
-                here = here + value
-                low = value.reshape(pack, LANES).astype(jnp.bfloat16)
-                weight[b, span, t * LANES : (t + 1) * LANES] = low
-            at = jnp.full((2, SUB, LANES), places[b], jnp.int32)
-            for w in range(3):
-                sums[w] = sums[w] + jnp.where(at == w, here, 0.0)
-        for w in range(3):
-            total[w, span, :] = sums[w].reshape(pack, LANES)
-        return carry
-
-    lax.fori_loop(0, size // pack, weigh, 0)
 
     mass = jnp.sum(total[...], axis=2, keepdims=True)
     mass = jnp.broadcast_to(mass, total.shape)
@@ -423,23 +432,17 @@
         )
 
     def numerators(n, carry):
+        products = []
+        for b in range(blocks):
+            product = jnp.dot(
+                weight[b],
+                feat[b * block_rows : (b + 1) * block_rows, columns(n)],
+                preferred_element_type=jnp.float32,
+            )
+            products.append((jnp.full(product.shape, places[b], jnp.int32), product))
         for w in range(3):
-            num_sum[n, w] = jnp.zeros((size, piece), jnp.float32)
-
-        def two_blocks(step, carry):
-            products = []
-            for b in (2 * step, 2 * step + 1):
-                span = pl.ds(pl.multiple_of(b * block_rows, block_rows), block_rows)
-                product = jnp.dot(
-                    weight[b], feat[span, columns(n)], preferred_element_type=jnp.float32
-                )
-                products.append((jnp.full(product.shape, places[b], jnp.int32), product))
-            for w in range(3):
-                kept = [jnp.where(at == w, product, 0.0) for at, product in products]
-                num_sum[n, w] = num_sum[n, w] + (kept[0] + kept[1])
-            return carry
-
-        lax.fori_loop(0, blocks // 2, two_blocks, 0)
+            kept = [jnp.where(at == w, product, 0.0) for at, product in products]
+            num_sum[n, w] = functools.reduce(jnp.add, kept)
         for s in range(2):
             num_src[s, n] = num_sum[n, 2 * ups[s]].astype(jnp.bfloat16)
             num_copy(s, n).start()

time: 120 us -> 118 us (0.983)
  Pallas kernels: 120 us -> 118 us
    pallas_call x1, Pallas kernels: 118 us -> 116 us  [local(): pl.pallas_call(functools.partial(kernel, n_dp, n_code), out_shape=(jax.Sh...]
where the time goes in v8:
time: 118 us
  Pallas kernels  118 us (100%)
    pallas_call x1, Pallas kernels, local(): pl.pallas_call(functools.partial(kernel, n_dp, n_code), out_shape=(jax.Sh...  116 us

profile of v8, /device:TPU:1, one launch (start us, length us, event | category | flops | bytes accessed | tf_op | source)
XLA Modules:
  0.0 118.2 jit_solution(680233965160842181)
XLA Ops:
  0.6 115.5 %balanced_kmeans.1 = (f32[3,256,256]{2,1,0:T(8,128)}, f32[2,128]{1,0:T(2,128)}) custom-call(s32[8,32]{1,0:T(8,128)} %lists_ref.1, bf16[4096,768]{1,0:T(8,128)(2,1)} %feat_hbm.1, bf16[256,768]{1,0:T(8,128)(2,1)} %cent_hbm.1), custom_call_target="tpu_custom_call" | custom-call | flops 6442450944 | bytes 7077888 | tf_op jit(solution)/shard_map/balanced_kmeans/pallas_call | solution.py:506
  116.1 2.0 %divide.1 = (bf16[256,768]{1,0:T(8,128)(2,1)}, f32[2,128]{1,0:T(2,128)}) custom-call(f32[3,256,256]{2,1,0:T(8,128)} %get-tuple-element.6.whole_ref, f32[2,128]{1,0:T(2,128)} %get-tuple-element.7.mass_in_ref), custom_call_target="tpu_custom_call" | custom-call | flops 196608 | bytes 1179648 | tf_op jit(solution)/shard_map/divide/pallas_call | solution.py:574

commit v9 on v8

--- a/solution.py
+++ b/solution.py
@@ -52,7 +52,7 @@
     mass_in,
     num_src,
     num_in,
-    num_sum,
+    num_own,
     feat_sem,
     own_sem,
     halo_send,
@@ -440,12 +440,15 @@
                 preferred_element_type=jnp.float32,
             )
             products.append((jnp.full(product.shape, places[b], jnp.int32), product))
-        for w in range(3):
+
+        def window_sum(w):
             kept = [jnp.where(at == w, product, 0.0) for at, product in products]
-            num_sum[n, w] = functools.reduce(jnp.add, kept)
+            return functools.reduce(jnp.add, kept).astype(jnp.bfloat16)
+
         for s in range(2):
-            num_src[s, n] = num_sum[n, 2 * ups[s]].astype(jnp.bfloat16)
+            num_src[s, n] = window_sum(2 * ups[s])
             num_copy(s, n).start()
+        num_own[n] = window_sum(1)
         return carry
 
     lax.fori_loop(0, PIECES, numerators, 0)
@@ -463,7 +466,7 @@
             remote(
                 num_src.at[s, n], num_in.at[s, n], num_send.at[s, n], num_recv.at[s, n], dp, code
             ).wait()
-        own = num_sum[n, 1].astype(jnp.bfloat16).astype(jnp.float32)
+        own = num_own[n].astype(jnp.float32)
         whole_ref[n] = (
             num_in[0, n].astype(jnp.float32) + own + num_in[1, n].astype(jnp.float32)
         )
@@ -543,7 +546,7 @@
                 pltpu.VMEM((2, 1, halves, LANES), f32),
                 pltpu.VMEM((2, PIECES, size, piece), bf16),
                 pltpu.VMEM((2, PIECES, size, piece), bf16),
-                pltpu.VMEM((PIECES, 3, size, piece), f32),
+                pltpu.VMEM((PIECES, size, piece), bf16),
                 dma((blocks,)),
                 dma,
                 dma((2,)),

time: 118 us -> 118 us (level)
  no operation moved by 1% of the time
where the time goes in v9:
time: 118 us
  Pallas kernels  118 us (100%)
    pallas_call x1, Pallas kernels, local(): pl.pallas_call(functools.partial(kernel, n_dp, n_code), out_shape=(jax.Sh...  116 us

profile of v9, /device:TPU:1, one launch (start us, length us, event | category | flops | bytes accessed | tf_op | source)
XLA Modules:
  0.0 118.2 jit_solution(654936609609711657)
XLA Ops:
  0.6 115.5 %balanced_kmeans.1 = (f32[3,256,256]{2,1,0:T(8,128)}, f32[2,128]{1,0:T(2,128)}) custom-call(s32[8,32]{1,0:T(8,128)} %lists_ref.1, bf16[4096,768]{1,0:T(8,128)(2,1)} %feat_hbm.1, bf16[256,768]{1,0:T(8,128)(2,1)} %cent_hbm.1), custom_call_target="tpu_custom_call" | custom-call | flops 6442450944 | bytes 7077888 | tf_op jit(solution)/shard_map/balanced_kmeans/pallas_call | solution.py:509
  116.1 2.0 %divide.1 = (bf16[256,768]{1,0:T(8,128)(2,1)}, f32[2,128]{1,0:T(2,128)}) custom-call(f32[3,256,256]{2,1,0:T(8,128)} %get-tuple-element.6.whole_ref, f32[2,128]{1,0:T(2,128)} %get-tuple-element.7.mass_in_ref), custom_call_target="tpu_custom_call" | custom-call | flops 196608 | bytes 1179648 | tf_op jit(solution)/shard_map/divide/pallas_call | solution.py:577
